TPU v7x, 128 devices: a whole 4x4x4 slice. The times are simulated.
128 devices in a mesh: grp: 8 (over z, core), mem: 16 (over y, x).
Axes of the slice: x: 4, y: 4, z: 4, core: 2. Of those that a mesh axis runs over, the one named last changes fastest.
Arguments:
- forcing: float32 [3, 1024, 4096], P(None, ('grp', 'mem')), may hold values from -6 to 6
- viscosity: float32 [1024, 4096], P(('grp', 'mem')), may hold values from 0.1 to 10
- refinement: int32 [1024], P(('grp', 'mem')), may hold values from 0 to 1
- face_owner: int32 [4096, 1], P(('grp', 'mem')), may hold values from 0 to 15; in each aligned block of 32 rows (0 to 31, 32 to 63, ...) at most 4 rows name the same one
- face_block: int32 [1024, 4], P(('grp', 'mem')), may hold values from 0 to 7
- plane_block: int32 [1024, 2], P(('grp', 'mem')), may hold values from 0 to 7
- hanging: int32 [1024, 6], P(('grp', 'mem')), may hold values 0 or 1
- coarse_solver: float32 [8, 384, 384], P('grp', 'mem'), may hold values from -0.3125 to 0.3125
Outputs:
- velocity: float32 [3, 1024, 4096], P(None, ('grp', 'mem'))
- residual: float32 [3, 1024, 4096], P(None, ('grp', 'mem'))
Inputs may be any that keep to these rules, and one draw needn't show every extreme that they name: `face_owner`: among the 32 rows of one device no member appears more than 4 times, and some member appears exactly 4 times.
All inputs are finite; a program needn't handle non-finite values. No bound on the sum of `hanging` on one device may be relied on, other than what follows from the above.
Results may differ from a plain program's by a relative error of at most 0.0001.
Values sent between devices are 32-bit elements; how exact they have to be, the bound alone decides.
A program may use at most 64 MiB of HBM per device.

v0:
```python
import math

import jax
import jax.numpy as jnp
from jax import lax
from jax.sharding import PartitionSpec as P

EDGE = 16
DEG = 3
CELLS = 4096
FACE = 256


MASS_TERM = 1.0
LOWER_BOUND = 0.25
UPPER_BOUND = 2.0
HIGHEST = lax.Precision.HIGHEST


def shifted_2(block, axis, distance):
    devices = range(lax.axis_size(axis))
    route = [(i - distance, i) for i in devices if i - distance in devices]
    return lax.ppermute(block, axis, route)


def coarsen(plane_vals):
    leading = plane_vals.shape[:-1]
    squares = plane_vals.reshape(leading + (EDGE // 2, 2, EDGE // 2, 2))
    average = jnp.mean(squares, axis=(-3, -1), keepdims=True)
    return jnp.broadcast_to(average, squares.shape).reshape(leading + (FACE,))


def tables():
    lanes = jnp.arange(FACE, dtype=jnp.int32)
    lane_k = lanes % EDGE
    lane_j = lanes // EDGE
    sources = [lanes - 1, lanes + 1, lanes - EDGE, lanes + EDGE]
    valid = [lane_k > 0, lane_k < EDGE - 1, lane_j > 0, lane_j < EDGE - 1]
    shift_mat = jnp.concatenate(
        [
            ((lanes[:, None] == sources[d][None, :]) & valid[d][None, :]).astype(jnp.float32)
            for d in range(4)
        ],
        axis=1,
    )
    places = jnp.arange(EDGE, dtype=jnp.int32)
    picks = [places * EDGE, places * EDGE + EDGE - 1, places, (EDGE - 1) * EDGE + places]
    pick_mats = [(lanes[:, None] == picks[d][None, :]).astype(jnp.float32) for d in range(4)]
    return (shift_mat, pick_mats)


def far_faces(upper_planes, lower_planes, plane_block):
    arrived = []
    for by_step, outgoing in ((1, upper_planes), (-1, lower_planes)):
        arrived.append(shifted_2(outgoing, "grp", by_step))
    lower_ghost = jnp.take(arrived[0], plane_block[:, 0], axis=1)
    upper_ghost = jnp.take(arrived[1], plane_block[:, 1], axis=1)
    return (lower_ghost, upper_ghost)


def local(
    forcing, viscosity, refinement, face_owner, face_block, plane_block, hanging, coarse_solver
):
    blocks_here = forcing.shape[1]
    shift_mat, pick_mats = tables()
    pick_all = jnp.concatenate(pick_mats, axis=1)
    forcing_cube = forcing.reshape(3, blocks_here, EDGE, FACE)
    effective = (
        viscosity.reshape(blocks_here, EDGE, FACE)
        * jnp.exp2(-refinement.astype(jnp.float32))[:, None, None]
    )
    owners = face_owner[:, 0]
    opposite = jnp.array([1, 0, 3, 2], jnp.int32)
    wanted = (face_block * 4 + opposite[None, :]).reshape(-1)

    def near_faces(face_rows):
        gathered = lax.all_gather(face_rows, "mem", axis=0, tiled=True)
        return gathered[owners * (4 * blocks_here) + wanted]

    def ghost_set(stacked):
        channels = stacked.shape[0]
        picked = jnp.einsum("cbil,lm->cbim", stacked, pick_all, precision=HIGHEST)
        face_rows = (
            picked.reshape(channels, blocks_here, EDGE, 4, EDGE)
            .transpose(1, 3, 0, 2, 4)
            .reshape(blocks_here * 4, channels * FACE)
        )
        ghost_rows = near_faces(face_rows).reshape(blocks_here, 4, channels, FACE)
        result = [ghost_rows[:, direction].transpose(1, 0, 2) for direction in range(4)]
        lower_ghost, upper_ghost = far_faces(
            stacked[:, :, EDGE - 1, :], stacked[:, :, 0, :], plane_block
        )
        result.append(lower_ghost)
        result.append(upper_ghost)
        return [
            jnp.where(
                hanging[:, direction][None, :, None] == 1,
                coarsen(result[direction]),
                result[direction],
            )
            for direction in range(6)
        ]

    def beside(values, ghosts):
        channels = values.shape[0]
        shifted = jnp.einsum("cbil,lm->cbim", values, shift_mat, precision=HIGHEST)
        nearby = []
        for direction in range(4):
            placed = jnp.einsum(
                "cbim,lm->cbil",
                ghosts[direction].reshape(channels, blocks_here, EDGE, EDGE),
                pick_mats[direction],
                precision=HIGHEST,
            )
            nearby.append(shifted[..., direction * FACE : (direction + 1) * FACE] + placed)
        nearby.append(jnp.concatenate([ghosts[4][:, :, None, :], values[:, :, :-1, :]], axis=2))
        nearby.append(jnp.concatenate([values[:, :, 1:, :], ghosts[5][:, :, None, :]], axis=2))
        return nearby

    nearby_eff = beside(effective[None], ghost_set(effective[None]))
    weights = [0.5 * (effective + nearby_eff[direction][0]) for direction in range(6)]
    diagonal = MASS_TERM * effective
    for direction in range(6):
        diagonal = diagonal + weights[direction]

    def operate(values):
        nearby = beside(values, ghost_set(values))
        applied = diagonal * values
        for direction in range(6):
            applied = applied - weights[direction] * nearby[direction]
        return applied

    midpoint = 0.5 * (UPPER_BOUND + LOWER_BOUND)
    half_width = 0.5 * (UPPER_BOUND - LOWER_BOUND)
    sigma_ratio = midpoint / half_width

    def smooth(solution, residual):
        rho_now = 1.0 / sigma_ratio
        step_dir = residual / (diagonal * midpoint)
        for sweep_index in range(DEG):
            solution = solution + step_dir
            residual = residual - operate(step_dir)
            if sweep_index < DEG - 1:
                rho_next = 1.0 / (2.0 * sigma_ratio - rho_now)
                step_dir = rho_next * rho_now * step_dir + 2.0 * rho_next / half_width * (
                    residual / diagonal
                )
                rho_now = rho_next
        return (solution, residual)

    solution, residual = smooth(jnp.zeros_like(forcing_cube), forcing_cube)
    coarse_local = (jnp.sum(residual, axis=(2, 3)) / math.sqrt(CELLS)).T.reshape(-1)
    rows_here = coarse_solver[0]
    correction = jnp.dot(
        rows_here,
        lax.all_gather(coarse_local, "mem", axis=0, tiled=True),
        precision=HIGHEST,
        preferred_element_type=jnp.float32,
    )
    lifted = jnp.broadcast_to(
        correction.reshape(blocks_here, 3).T[:, :, None, None], forcing_cube.shape
    )
    solution = solution + lifted
    residual = residual - operate(lifted)
    solution, residual = smooth(solution, residual)
    return (solution.reshape(forcing.shape), residual.reshape(forcing.shape))


def solution(mesh):
    in_specs = (
        P(None, ("grp", "mem"), None),
        P(("grp", "mem"), None),
        P(("grp", "mem")),
        P(("grp", "mem"), None),
        P(("grp", "mem"), None),
        P(("grp", "mem"), None),
        P(("grp", "mem"), None),
        P("grp", "mem", None),
    )
    out_specs = (P(None, ("grp", "mem"), None), P(None, ("grp", "mem"), None))
    return jax.shard_map(local, mesh=mesh, in_specs=in_specs, out_specs=out_specs, check_vma=False)
```

profile of v0, /device:TPU:0, one launch (start us, length us, event | category | flops | bytes accessed | tf_op | source)
XLA Modules:
  0.0 609.0 jit_solution(15840290535157774675)
XLA Ops:
  14.4 24.8 %all_gather.27 = f32[512,256]{1,0:T(8,128)S(1)} all-gather(f32[32,256]{1,0:T(8,128)S(1)} %reshape.1007), channel_id=1, replica_groups=mesh['grp'=8,'mem'=16] {'mem'}, dimensions={0}, use_global_device_ids=true | all-gather | bytes 557056 | tf_op jit(solution)/shard_map/all_gather | solution.py:77
  71.7 25.1 %all-gather.8.cloned.1.call-done = f32[512,768]{1,0:T(8,128)} async-done(((f32[32,768]{1,0:T(8,128)}), f32[512,768]{1,0:T(8,128)}) %all-gather.8.cloned.1.call-update) | async-done | bytes 1572880 | tf_op jit(solution)/shard_map/all_gather | solution.py:77
  96.8 2.2 gather_fusion.1
  129.6 2.1 gather_fusion.12
  134.8 2.0 reduce_sum.457
  143.1 2.0 gather_fusion.13
  148.2 1.9 reduce_sum.458
  155.1 11.8 %all-gather.10.cloned.1.call-done = f32[512,768]{1,0:T(8,128)} async-done(((f32[32,768]{1,0:T(8,128)}), f32[512,768]{1,0:T(8,128)}) %all-gather.10.cloned.1.call-update) | async-done | bytes 1572880 | tf_op jit(solution)/shard_map/all_gather | solution.py:77
  166.9 2.8 gather_fusion.2
  174.5 2.0 reduce_sum.453
  181.6 2.0 reduce_sum.454
  188.8 2.0 reduce_sum.455
  195.9 1.9 reduce_sum.456
  226.6 2.0 fusion.97
  236.6 28.6 %all-gather.12.cloned.1.call-done = f32[512,768]{1,0:T(8,128)} async-done(((f32[32,768]{1,0:T(8,128)}), f32[512,768]{1,0:T(8,128)}) %all-gather.12.cloned.1.call-update) | async-done | bytes 1572880 | tf_op jit(solution)/shard_map/all_gather | solution.py:77
  265.2 2.2 gather_fusion.3
  281.8 38.1 %all-reduce = f32[384]{0:T(512)S(1)} all-reduce(f32[384]{0:T(512)S(1)} %dynamic-update-slice), channel_id=1, replica_groups=mesh['grp'=8,'mem'=16] {'mem'}, use_global_device_ids=true, to_apply=%add | all-reduce | flops 384 | bytes 3072
  321.7 2.1 reshape.1069
  325.3 2.0 fusion.95
  334.6 29.6 %all-gather.14.cloned.1.call-done = f32[512,768]{1,0:T(8,128)} async-done(((f32[32,768]{1,0:T(8,128)}), f32[512,768]{1,0:T(8,128)}) %all-gather.14.cloned.1.call-update) | async-done | bytes 1572880 | tf_op jit(solution)/shard_map/all_gather | solution.py:77
  364.2 2.2 gather_fusion.4
  381.7 2.0 fusion.93
  402.3 21.4 %all-gather.16.cloned.1.call-done = f32[512,768]{1,0:T(8,128)} async-done(((f32[32,768]{1,0:T(8,128)}), f32[512,768]{1,0:T(8,128)}) %all-gather.16.cloned.1.call-update) | async-done | bytes 1572880 | tf_op jit(solution)/shard_map/all_gather | solution.py:77
  423.7 2.2 gather_fusion.5
  451.2 2.1 copy.658
  453.4 2.1 reshape.1107
  456.8 2.0 fusion.91
  477.6 21.2 %all-gather.18.cloned.1.call-done = f32[512,768]{1,0:T(8,128)} async-done(((f32[32,768]{1,0:T(8,128)}), f32[512,768]{1,0:T(8,128)}) %all-gather.18.cloned.1.call-update) | async-done | bytes 1572880 | tf_op jit(solution)/shard_map/all_gather | solution.py:77
  498.8 2.2 gather_fusion.6
  527.5 1.9 collective-permute-start.14
  548.0 22.2 %all-gather.20.cloned.1.call-done = f32[512,768]{1,0:T(8,128)} async-done(((f32[32,768]{1,0:T(8,128)}), f32[512,768]{1,0:T(8,128)}) %all-gather.20.cloned.1.call-update) | async-done | bytes 1572880 | tf_op jit(solution)/shard_map/all_gather | solution.py:77
  570.2 2.2 gather_fusion.7
  (868 shorter events, 319.2 us)
Async XLA Ops:
  7.2 32.1 %copy-start.144 = (s32[4]{0:T(128)S(1)}, s32[4]{0:T(128)}, u32[]{:S(2)}) copy-start(s32[4]{0:T(128)} %constant.145.clone) | copy-start | bytes 52
  7.2 32.0 %copy-start.142 = (s32[8,4]{0,1:T(4,128)S(1)}, s32[8,4]{0,1:T(4,128)}, u32[]{:S(2)}) copy-start(s32[8,4]{0,1:T(4,128)} %param.17) | copy-start | bytes 388
  7.2 32.3 %copy-start.145 = (s32[32,1]{0,1:T(1,128)S(1)}, s32[32,1]{0,1:T(1,128)}, u32[]{:S(2)}) copy-start(s32[32,1]{0,1:T(1,128)} %param.16) | copy-start | bytes 388
  7.2 89.6 %all-gather.8.cloned.1.call-start = ((), (), s32[]{:S(2)}) async-start(), calls=%async_computation | async-start | bytes 1671168 | tf_op jit(solution)/shard_map/all_gather | solution.py:77
  7.9 39.1 %copy-start.140 = (f32[8]{0:T(128)}, f32[8]{0:T(128)S(1)}, u32[]{:S(2)}) copy-start(f32[8]{0:T(128)S(1)} %multiply_exponential_fusion) | copy-start | bytes 100
  8.9 35.8 %collective-permute-start = (f32[1,8,256]{2,0,1:T(1,128)S(1)}, f32[1,8,256]{2,0,1:T(1,128)S(1)}, u32[]{:S(2)}, u32[]{:S(2)}) collective-permute-start(f32[1,8,256]{2,0,1:T(1,128)S(1)} %get-tuple-element.104), channel_id=1, source_target_pairs={{0,16},{16,32},{32,48},{48,64},{64,80},{80,96},{96,112},{1,17},{17... | collective-permute-start | bytes 24584 | tf_op jit(solution)/shard_map/ppermute | solution.py:23
  10.2 35.6 %collective-permute-start.1 = (f32[1,8,256]{2,0,1:T(1,128)S(1)}, f32[1,8,256]{2,0,1:T(1,128)S(1)}, u32[]{:S(2)}, u32[]{:S(2)}) collective-permute-start(f32[1,8,256]{2,0,1:T(1,128)S(1)} %get-tuple-element.105), channel_id=1, source_target_pairs={{16,0},{32,16},{48,32},{64,48},{80,64},{96,80},{112,96},{17,1},{33... | collective-permute-start | bytes 24584 | tf_op jit(solution)/shard_map/ppermute | solution.py:23
  11.5 32.2 %copy-start.129 = (s32[16]{0:T(128)}, s32[16]{0:T(128)S(1)}, u32[]{:S(2)}) copy-start(s32[16]{0:T(128)S(1)} %iota_add_fusion.4) | copy-start | bytes 196
  11.5 31.4 %copy-start.122 = (s32[16]{0:T(128)}, s32[16]{0:T(128)S(1)}, u32[]{:S(2)}) copy-start(s32[16]{0:T(128)S(1)} %broadcast_add_fusion) | copy-start | bytes 196
  49.6 117.3 %all-gather.10.cloned.1.call-start = ((), (), s32[]{:S(2)}) async-start(), calls=%async_computation.1 | async-start | bytes 1671168 | tf_op jit(solution)/shard_map/all_gather | solution.py:77
  49.9 5.5 collective-permute-start.2
  51.8 11.4 %collective-permute-start.3 = (f32[3,8,256]{2,1,0:T(8,128)}, f32[3,8,256]{2,1,0:T(8,128)}, u32[]{:S(2)}, u32[]{:S(2)}) collective-permute-start(f32[3,8,256]{2,1,0:T(8,128)} %bitcast.760), channel_id=1, source_target_pairs={{16,0},{32,16},{48,32},{64,48},{80,64},{96,80},{112,96},{17,1},{33... | collective-permute-start | bytes 73736 | tf_op jit(solution)/shard_map/ppermute | solution.py:23
  123.6 141.7 %all-gather.12.cloned.1.call-start = ((), (), s32[]{:S(2)}) async-start(), calls=%async_computation.2 | async-start | bytes 1671168 | tf_op jit(solution)/shard_map/all_gather | solution.py:77
  123.7 5.3 collective-permute-start.4
  125.8 89.8 %copy-start.1 = (f32[3,8,16,1024]{3,2,1,0:T(8,128)}, f32[3,8,16,1024]{3,2,1,0:T(8,128)S(1)}, u32[]{:S(2)}) copy-start(f32[3,8,16,1024]{3,2,1,0:T(8,128)S(1)} %fusion.99) | copy-start | bytes 4718596
  127.5 14.3 %collective-permute-start.5 = (f32[3,8,256]{2,1,0:T(8,128)}, f32[3,8,256]{2,1,0:T(8,128)}, u32[]{:S(2)}, u32[]{:S(2)}) collective-permute-start(f32[3,8,256]{2,1,0:T(8,128)} %bitcast.758), channel_id=1, source_target_pairs={{16,0},{32,16},{48,32},{64,48},{80,64},{96,80},{112,96},{17,1},{33... | collective-permute-start | bytes 73736 | tf_op jit(solution)/shard_map/ppermute | solution.py:23
  221.9 142.3 %all-gather.14.cloned.1.call-start = ((), (), s32[]{:S(2)}) async-start(), calls=%async_computation.3 | async-start | bytes 1671168 | tf_op jit(solution)/shard_map/all_gather | solution.py:77
  225.3 6.0 collective-permute-start.6
  229.5 4.9 collective-permute-start.7
  280.1 39.8 %copy-start.69 = (f32[8,3,384]{2,1,0:T(4,128)S(1)}, f32[8,3,384]{2,1,0:T(4,128)}, u32[]{:S(2)}) copy-start(f32[8,3,384]{2,1,0:T(4,128)} %dot_general.197) | copy-start | bytes 110596
  320.2 51.6 %copy-start.99 = (f32[1,8,3]{1,2,0:T(4,128)}, f32[1,8,3]{1,2,0:T(4,128)S(1)}, u32[]{:S(2)}) copy-start(f32[1,8,3]{1,2,0:T(4,128)S(1)} %copy.721) | copy-start | bytes 292
  323.8 99.9 %all-gather.16.cloned.1.call-start = ((), (), s32[]{:S(2)}) async-start(), calls=%async_computation.4 | async-start | bytes 1671168 | tf_op jit(solution)/shard_map/all_gather | solution.py:77
  324.0 4.9 collective-permute-start.8
  327.3 5.0 collective-permute-start.9
  380.3 118.5 %all-gather.18.cloned.1.call-start = ((), (), s32[]{:S(2)}) async-start(), calls=%async_computation.5 | async-start | bytes 1671168 | tf_op jit(solution)/shard_map/all_gather | solution.py:77
  380.4 6.2 %collective-permute-start.10 = (f32[3,8,256]{2,1,0:T(8,128)S(1)}, f32[3,8,256]{2,1,0:T(8,128)S(1)}, u32[]{:S(2)}, u32[]{:S(2)}) collective-permute-start(f32[3,8,256]{2,1,0:T(8,128)S(1)} %bitcast.936), channel_id=1, source_target_pairs={{0,16},{16,32},{32,48},{48,64},{64,80},{80,96},{96,112},{1,17},{17... | collective-permute-start | bytes 73736 | tf_op jit(solution)/shard_map/ppermute | solution.py:23
  385.1 8.6 %collective-permute-start.11 = (f32[3,8,256]{2,1,0:T(8,128)}, f32[3,8,256]{2,1,0:T(8,128)}, u32[]{:S(2)}, u32[]{:S(2)}) collective-permute-start(f32[3,8,256]{2,1,0:T(8,128)} %bitcast.754), channel_id=1, source_target_pairs={{16,0},{32,16},{48,32},{64,48},{80,64},{96,80},{112,96},{17,1},{33... | collective-permute-start | bytes 73736 | tf_op jit(solution)/shard_map/ppermute | solution.py:23
  455.4 114.8 %all-gather.20.cloned.1.call-start = ((), (), s32[]{:S(2)}) async-start(), calls=%async_computation.6 | async-start | bytes 1671168 | tf_op jit(solution)/shard_map/all_gather | solution.py:77
  455.6 6.4 %collective-permute-start.12 = (f32[3,8,256]{2,1,0:T(8,128)S(1)}, f32[3,8,256]{2,1,0:T(8,128)S(1)}, u32[]{:S(2)}, u32[]{:S(2)}) collective-permute-start(f32[3,8,256]{2,1,0:T(8,128)S(1)} %bitcast.937), channel_id=1, source_target_pairs={{0,16},{16,32},{32,48},{48,64},{64,80},{80,96},{96,112},{1,17},{17... | collective-permute-start | bytes 73736 | tf_op jit(solution)/shard_map/ppermute | solution.py:23
  460.4 8.7 %collective-permute-start.13 = (f32[3,8,256]{2,1,0:T(8,128)}, f32[3,8,256]{2,1,0:T(8,128)}, u32[]{:S(2)}, u32[]{:S(2)}) collective-permute-start(f32[3,8,256]{2,1,0:T(8,128)} %bitcast.752), channel_id=1, source_target_pairs={{16,0},{32,16},{48,32},{64,48},{80,64},{96,80},{112,96},{17,1},{33... | collective-permute-start | bytes 73736 | tf_op jit(solution)/shard_map/ppermute | solution.py:23
  527.5 7.5 %collective-permute-start.14 = (f32[3,8,256]{2,1,0:T(8,128)}, f32[3,8,256]{2,1,0:T(8,128)}, u32[]{:S(2)}, u32[]{:S(2)}) collective-permute-start(f32[3,8,256]{2,1,0:T(8,128)} %bitcast.751), channel_id=1, source_target_pairs={{0,16},{16,32},{32,48},{48,64},{64,80},{80,96},{96,112},{1,17},{17... | collective-permute-start | bytes 73736 | tf_op jit(solution)/shard_map/ppermute | solution.py:23
  530.0 6.5 %collective-permute-start.15 = (f32[3,8,256]{2,1,0:T(8,128)}, f32[3,8,256]{2,1,0:T(8,128)}, u32[]{:S(2)}, u32[]{:S(2)}) collective-permute-start(f32[3,8,256]{2,1,0:T(8,128)} %bitcast.750), channel_id=1, source_target_pairs={{16,0},{32,16},{48,32},{64,48},{80,64},{96,80},{112,96},{17,1},{33... | collective-permute-start | bytes 73736 | tf_op jit(solution)/shard_map/ppermute | solution.py:23
  (137 other events, 379.5 us)
Sparse Core Ops, SparseCore 0:
  49.8 46.9 all-gather.7
  123.7 43.1 all-gather.9
  222.0 43.1 all-gather.11
  324.0 40.1 all-gather.13
  380.4 43.1 all-gather.15
  455.6 43.1 all-gather.17
  527.0 43.1 all-gather.19
where the time goes:
time: 621 us; the launch traced here: 609 us
  local copies, waits for them, and re-layouts  207 us (33%)
  waiting for transfers between devices  162 us (26%)
  other arithmetic  92.3 us (15%)
  blocking collectives  62.9 us (10%)
  matrix products  41.7 us (7%)
  starting transfers between devices  23.6 us (4%)
  between operations  19.2 us (3%)
    all_gather x7, waiting for transfers between devices, near_faces(): gathered = lax.all_gather(face_rows, 'mem', axis=0, tiled=True)  160 us
    reduce_sum x48, other arithmetic, coarsen(): average = jnp.mean(squares, axis=(-3, -1), keepdims=True)  42 us
    unnamed x1, blocking collectives  38.1 us
    reshape x42, local copies, waits for them, and re-layouts, coarsen(): return jnp.broadcast_to(average, squares.shape).reshape(leading + (FACE,))  35.4 us
    transpose x35, local copies, waits for them, and re-layouts, ghost_set(): ghost_rows[:, direction].transpose(1, 0, 2)  31.4 us
    dot_general x32, matrix products, beside(): jnp.einsum('cbim,lm->cbil', ghosts[direction].reshape(channels, blocks_he...  27.8 us
    all_gather x1, blocking collectives, near_faces(): gathered = lax.all_gather(face_rows, 'mem', axis=0, tiled=True)  24.8 us
    ppermute x16, starting transfers between devices, shifted_2(): return lax.ppermute(block, axis, route)  23.3 us
  transfers between devices with their start and end apart: 23, of which 9 were waited for; matrix products, arithmetic and copies ran while one was open for 20% of the time, Pallas kernels for 0%

commit v1 on v0

v1 whole, which is shorter than its diff:
```python
import functools
import math

import jax
import jax.numpy as jnp
from jax import lax
from jax.experimental import pallas as pl
from jax.experimental.pallas import tpu as pltpu
from jax.sharding import PartitionSpec as P

MESH = pl.DeviceIdType.MESH
EDGE = 16
DEG = 3
CELLS = 4096
FACE = 256
LANES = 128
CAP = 4
MASS_TERM = 1.0
LOWER_BOUND = 0.25
UPPER_BOUND = 2.0
SWEEPS = 2 * DEG
F32 = jnp.float32
BF16 = jnp.bfloat16
REQUEST, EFFECTIVE, CORRECTION = 0, 1, 2


def chebyshev():
    theta = 0.5 * (UPPER_BOUND + LOWER_BOUND)
    delta = 0.5 * (UPPER_BOUND - LOWER_BOUND)
    sigma = theta / delta
    rho = 1.0 / sigma
    steps = [(0.0, 1.0 / theta)]
    for _ in range(DEG - 1):
        rho_next = 1.0 / (2.0 * sigma - rho)
        steps.append((rho_next * rho, 2.0 * rho_next / delta))
        rho = rho_next
    return steps


def by_step(step, values):
    result = jnp.float32(values[-1])
    for place in range(len(values) - 2, -1, -1):
        result = jnp.where(step == place, jnp.float32(values[place]), result)
    return result


def iota(shape, dim):
    return lax.broadcasted_iota(jnp.int32, shape, dim)


def turn(x, shift):
    shift = shift % LANES
    return x if shift == 0 else pltpu.roll(x, shift, 1)


def part(i, v):
    return pl.ds(i * FACE + v * LANES, LANES)


def pick(one_hot, values):
    high = values.astype(BF16)
    rest = values - high.astype(F32)
    middle = rest.astype(BF16)
    low = (rest - middle.astype(F32)).astype(BF16)

    def product(piece):
        return jnp.dot(one_hot, piece, preferred_element_type=F32)

    return product(high) + (product(middle) + product(low))


def coarsen(x):
    lane = iota(x.shape, 1)
    x = x + jnp.where(lane % 2 == 0, turn(x, -1), turn(x, 1))
    x = x + jnp.where(lane // EDGE % 2 == 0, turn(x, -EDGE), turn(x, EDGE))
    return 0.25 * x


def extract(read):
    lane = iota((8, LANES), 1)
    in_row, row = lane % EDGE, lane // EDGE
    zero = jnp.zeros((8, LANES), F32)
    faces = {(v, d): zero for v in range(2) for d in range(4)}
    for i in range(EDGE):
        halves = (read(i, 0), read(i, 1))
        for v in range(2):
            moved = turn(halves[v], i)
            faces[v, 0] = jnp.where(in_row == i, moved, faces[v, 0])
            faces[v, 1] = jnp.where(in_row == (i - 1) % EDGE, moved, faces[v, 1])
        v = i // 8
        moved = turn(jnp.where(lane < EDGE, halves[0], halves[1]), i % 8 * EDGE)
        faces[v, 2] = jnp.where(row == i % 8, moved, faces[v, 2])
        faces[v, 3] = jnp.where(row == (i - 1) % 8, moved, faces[v, 3])
    for v in range(2):
        faces[v, 1] = turn(faces[v, 1], -(EDGE - 1))
        faces[v, 3] = turn(faces[v, 3], EDGE)
    return faces


def tables(owner, face_block, plane_block, hanging, members, has_lower, has_upper):
    wide = members * 8
    rows, columns = iota((32, 32), 0), iota((32, 32), 1)
    given = 4 * (rows % 8) + rows // 8
    given_t = 4 * (columns % 8) + columns // 8
    across = jnp.sum(jnp.where(rows == columns, owner, 0), axis=0, keepdims=True)
    owner_col = jnp.sum(jnp.where(columns == given, across, 0), axis=1, keepdims=True)
    owner_row = jnp.sum(jnp.where(rows == given_t, owner, 0), axis=0, keepdims=True)
    same = owner_col == owner_row
    rank_col = jnp.sum(jnp.where(same & (columns < rows), 1, 0), axis=1, keepdims=True)
    rank_row = jnp.sum(jnp.where(same & (rows < columns), 1, 0), axis=0, keepdims=True)

    def spread(table, first, groups, of_row):
        tall = jnp.concatenate([table] * groups, axis=0)
        mask = iota(tall.shape, 1) == first + of_row(iota(tall.shape, 0))
        return jnp.sum(jnp.where(mask, tall, 0), axis=1, keepdims=True)

    block_col = spread(face_block, 0, 4, lambda r: r // 8)
    side = iota((32, 1), 0) // 8
    wanted = (side + 1 - 2 * (side % 2)) * 8 + block_col
    slot_col = owner_col * 8 + rank_col
    slot_row = owner_row * 8 + rank_row

    def ones(mask):
        return jnp.where(mask, 1.0, 0.0).astype(BF16)

    lanes = iota((32, wide), 1)
    unpack = jnp.concatenate([ones(lanes == slot_col + CAP * v) for v in range(2)], axis=0)
    slots = iota((wide, 32), 0)
    unpack_t = jnp.concatenate([ones(slots == slot_row + CAP * v) for v in range(2)], axis=1)
    lanes = iota((32, LANES), 1)
    source = jnp.concatenate([ones(lanes == wanted + 32 * v) for v in range(2)], axis=0)
    request = jnp.dot(unpack_t, source, preferred_element_type=F32)
    plane_col = spread(plane_block, 0, 4, lambda r: r // 16)
    which = iota((32, 32), 0) // 16
    inside = jnp.where(which == 0, has_lower, has_upper) == 1
    plane_pick = ones((columns == rows // 8 * 8 + plane_col) & inside)
    lift_pick = ones(iota((32, wide), 1) == owner_col * 8 + block_col)
    near_hang = spread(hanging, 0, 4, lambda r: r // 8)
    plane_hang = spread(hanging, 4, 4, lambda r: r // 16)
    near_hang = jnp.broadcast_to(near_hang.astype(F32), (32, LANES))
    plane_hang = jnp.broadcast_to(plane_hang.astype(F32), (32, LANES))
    return unpack, request, plane_pick, lift_pick, near_hang, plane_hang


def kernel(
    n_grp,
    n_mem,
    forcing,
    viscosity,
    refinement,
    face_owner,
    face_block,
    plane_block,
    hanging,
    coarse_solver,
    velocity,
    residual,
    effective,
    weight_k,
    weight_j,
    weight_i,
    ghost_k,
    ghost_j,
    diagonal,
    inverse,
    step_dir,
    faces,
    ghosts,
    plane_ghosts,
    hang_near,
    hang_plane,
    unpack_mat,
    pack_mat,
    plane_mat,
    lift_mat,
    solver_rows,
    out_big,
    in_big,
    out_small,
    in_small,
    out_plane,
    in_plane,
    send_big,
    recv_big,
    send_small,
    recv_small,
    send_plane,
    recv_plane,
):
    grp, mem = lax.axis_index("grp"), lax.axis_index("mem")
    above = lax.rem(grp + 1, n_grp)
    below = lax.rem(grp + n_grp - 1, n_grp)
    n_coarse = n_mem * 24
    groups_of_lanes = -(-n_coarse // LANES)
    wide = n_mem * 8
    COARSE = SWEEPS

    barrier = pltpu.get_barrier_semaphore()
    for offset in range(1, n_mem):
        pl.semaphore_signal(
            barrier, inc=1, device_id={"mem": lax.rem(mem + offset, n_mem)}, device_id_type=MESH
        )
    for other in (above, below):
        pl.semaphore_signal(barrier, inc=1, device_id={"grp": other}, device_id_type=MESH)

    lane = iota((8, LANES), 1)
    in_row = lane % EDGE
    first_k, last_k = in_row == 0, in_row == EDGE - 1
    first_row, last_row = lane < EDGE, lane >= LANES - EDGE

    def send(outgoing, incoming, which, send_sem, recv_sem):
        for offset in range(1, n_mem):
            to = lax.rem(mem + offset, n_mem)
            pltpu.make_async_remote_copy(
                src_ref=outgoing.at[which, to],
                dst_ref=incoming.at[which, mem],
                send_sem=send_sem.at[which],
                recv_sem=recv_sem.at[which],
                device_id={"mem": to},
                device_id_type=MESH,
            ).start()

    def all_of(buffer, which, sem):
        span = buffer.at[which, pl.ds(0, n_mem - 1)]
        pltpu.make_async_copy(span, span, sem.at[which]).wait()

    def plane_copy(which, side):
        return pltpu.make_async_remote_copy(
            src_ref=out_plane.at[which, side],
            dst_ref=in_plane.at[which, side],
            send_sem=send_plane.at[which, side],
            recv_sem=recv_plane.at[which, side],
            device_id={"grp": above if side == 0 else below},
            device_id_type=MESH,
        )

    unpack, request, plane_pick, lift_pick, near_hang, plane_hang = tables(
        face_owner[...],
        face_block[...],
        plane_block[...],
        hanging[...],
        n_mem,
        jnp.where(grp > 0, 1, 0),
        jnp.where(grp < n_grp - 1, 1, 0),
    )
    unpack_mat[...] = unpack
    plane_mat[...] = plane_pick
    lift_mat[...] = lift_pick
    hang_near[...] = near_hang
    hang_plane[...] = plane_hang
    out_small[REQUEST] = request.reshape(n_mem, 8, LANES)

    pl.semaphore_wait(barrier, n_mem - 1 + 2)

    send(out_small, in_small, REQUEST, send_small, recv_small)
    in_small[REQUEST, mem] = out_small[REQUEST, mem]

    block_row = iota((8, LANES), 0)
    level = jnp.zeros((8, LANES), jnp.int32)
    for b in range(8):
        level = jnp.where(block_row == b, refinement[b], level)
    scale = 1.0 / jnp.left_shift(jnp.ones_like(level), level).astype(F32)
    for i in range(EDGE):
        for v in range(2):
            effective[:, part(i, v)] = viscosity[:, part(i, v)] * scale

    def send_planes(which, channels, read):
        for c in range(channels):
            for v in range(2):
                out_plane[which, 0, c, pl.ds(8 * v, 8), :] = read(c, EDGE - 1, v)
                out_plane[which, 1, c, pl.ds(8 * v, 8), :] = read(c, 0, v)
        for side in range(2):
            plane_copy(which, side).start()

    for side in range(2):
        for c in range(1, 3):
            out_plane[SWEEPS, side, c] = jnp.zeros((16, LANES), F32)
    send_planes(SWEEPS, 1, lambda c, i, v: effective[:, part(i, v)])
    found = extract(lambda i, v: effective[:, part(i, v)])
    for (v, d), register in found.items():
        faces[0, pl.ds(v * 32 + d * 8, 8), :] = register

    all_of(in_small, REQUEST, recv_small)
    pack_mat[...] = in_small[REQUEST].reshape(wide, LANES)[:, :64].astype(BF16)
    out_small[EFFECTIVE] = pick(pack_mat[...], faces[0]).reshape(n_mem, 8, LANES)
    send(out_small, in_small, EFFECTIVE, send_small, recv_small)
    in_small[EFFECTIVE, mem] = out_small[EFFECTIVE, mem]

    rows, columns = iota((24, 24), 0), iota((24, 24), 1)
    reorder = jnp.where(columns == 3 * (rows % 8) + rows // 8, 1.0, 0.0).astype(BF16)
    solver_rows[:, pl.ds(0, n_coarse)] = pick(reorder, coarse_solver[0])
    if n_coarse % LANES:
        spare = groups_of_lanes * LANES - n_coarse
        solver_rows[:, pl.ds(n_coarse, spare)] = jnp.zeros((24, spare), F32)
    for c in range(3):
        for i in range(EDGE):
            for v in range(2):
                residual[c, :, part(i, v)] = forcing[c, :, part(i, v)]
                velocity[c, :, part(i, v)] = jnp.zeros((8, LANES), F32)
                step_dir[c, :, part(i, v)] = jnp.zeros((8, LANES), F32)
    for i in range(EDGE):
        own = [effective[:, part(i, v)] for v in range(2)]
        back = [turn(x, EDGE) for x in own]
        ahead = [turn(x, -EDGE) for x in own]
        for v in range(2):
            x = own[v]
            lower_k = jnp.where(first_k, 0.0, 0.5 * (x + turn(x, 1)))
            upper_k = jnp.where(last_k, 0.0, 0.5 * (x + turn(x, -1)))
            if v == 0:
                lower_j = jnp.where(first_row, 0.0, 0.5 * (x + back[0]))
                upper_j = 0.5 * (x + jnp.where(last_row, ahead[1], ahead[0]))
            else:
                lower_j = 0.5 * (x + jnp.where(first_row, back[0], back[1]))
                upper_j = jnp.where(last_row, 0.0, 0.5 * (x + ahead[1]))
            weight_k[0, :, part(i, v)] = lower_k
            weight_k[1, :, part(i, v)] = upper_k
            weight_j[0, :, part(i, v)] = lower_j
            weight_j[1, :, part(i, v)] = upper_j
            if i > 0:
                weight_i[:, part(i, v)] = 0.5 * (x + effective[:, part(i - 1, v)])
            diagonal[:, part(i, v)] = MASS_TERM * x + lower_k + upper_k + lower_j + upper_j

    def settle(values, hang):
        return jnp.where(hang == 1.0, coarsen(values), values)

    def side_by_side(buffer, channels):
        return jnp.concatenate([buffer(c) for c in range(channels)], axis=1)

    def receive_planes(which, channels):
        for side in range(2):
            plane_copy(which, side).wait_recv()
        arrived = side_by_side(
            lambda c: in_plane[which, :, c].reshape(32, LANES), channels
        )
        picked = pick(plane_mat[...], arrived)
        for c in range(channels):
            plane_ghosts[c] = settle(picked[:, c * LANES : (c + 1) * LANES], hang_plane[...])

    def unpack_near(arrived, channels):
        picked = pick(unpack_mat[...], arrived)
        for c in range(channels):
            for v in range(2):
                ghosts[c, pl.ds(32 * v, 32), :] = settle(
                    picked[32 * v : 32 * v + 32, c * LANES : (c + 1) * LANES], hang_near[...]
                )

    def ghost(c, d, v):
        return ghosts[c, pl.ds(v * 32 + d * 8, 8), :]

    def plane_ghost(c, side, v):
        return plane_ghosts[c, pl.ds(side * 16 + v * 8, 8), :]

    def k_ghost(c, i, v):
        return jnp.where(first_k, turn(ghost(c, 0, v), -i), turn(ghost(c, 1, v), EDGE - 1 - i))

    def j_ghost(c, i, v):
        shift = -(i % 8) * EDGE
        if v == 0:
            return turn(ghost(c, 2, i // 8), shift)
        return turn(ghost(c, 3, i // 8), LANES - EDGE + shift)

    receive_planes(SWEEPS, 1)
    for v in range(2):
        weight_i[:, part(0, v)] = 0.5 * (effective[:, part(0, v)] + plane_ghost(0, 0, v))
        weight_i[:, part(EDGE, v)] = 0.5 * (effective[:, part(EDGE - 1, v)] + plane_ghost(0, 1, v))
    all_of(in_small, EFFECTIVE, recv_small)
    unpack_near(in_small[EFFECTIVE].reshape(wide, LANES), 1)
    for i in range(EDGE):
        for v in range(2):
            x = effective[:, part(i, v)]
            at_k = jnp.where(first_k | last_k, 0.5 * (x + k_ghost(0, i, v)), 0.0)
            edge = first_row if v == 0 else last_row
            at_j = jnp.where(edge, 0.5 * (x + j_ghost(0, i, v)), 0.0)
            ghost_k[:, part(i, v)] = at_k
            ghost_j[:, part(i, v)] = at_j
            whole = (
                diagonal[:, part(i, v)]
                + (weight_i[:, part(i, v)] + weight_i[:, part(i + 1, v)])
                + (at_k + at_j)
            )
            diagonal[:, part(i, v)] = whole
            inverse[:, part(i, v)] = 1.0 / whole

    steps = chebyshev()

    def coarse_level():
        totals = []
        for c in range(3):
            total = jnp.zeros((8, LANES), F32)
            for i in range(EDGE):
                for v in range(2):
                    total = total + residual[c, :, part(i, v)]
            totals.append(jnp.sum(total, axis=1, keepdims=True) / math.sqrt(CELLS))
        for q in range(groups_of_lanes):
            place = lane + q * LANES - 24 * mem - 3 * block_row
            mine = jnp.zeros((8, LANES), F32)
            for c in range(3):
                mine = jnp.where(place == c, totals[c], mine)
            for m in range(n_mem):
                out_big[COARSE, m, q] = mine
        for q in range(groups_of_lanes, 3):
            for m in range(n_mem):
                out_big[COARSE, m, q] = jnp.zeros((8, LANES), F32)
        send(out_big, in_big, COARSE, send_big, recv_big)
        in_big[COARSE, mem] = out_big[COARSE, mem]
        all_of(in_big, COARSE, recv_big)
        products = [jnp.zeros((8, LANES), F32)] * 3
        for q in range(groups_of_lanes):
            vector = in_big[COARSE, 0, q]
            for m in range(1, n_mem):
                vector = vector + in_big[COARSE, m, q]
            vector = jnp.sum(vector, axis=0, keepdims=True)
            for c in range(3):
                products[c] = products[c] + solver_rows[
                    pl.ds(8 * c, 8), pl.ds(q * LANES, LANES)
                ] * vector
        own = [jnp.sum(products[c], axis=1, keepdims=True) for c in range(3)]
        tile = jnp.zeros((8, LANES), F32)
        for c in range(3):
            tile = jnp.where(lane == c, own[c], tile)
        for m in range(n_mem):
            out_small[CORRECTION, m] = tile
        send(out_small, in_small, CORRECTION, send_small, recv_small)
        in_small[CORRECTION, mem] = tile
        for side in range(2):
            for c in range(3):
                out_plane[SWEEPS + 1, side, c] = jnp.concatenate([tile, tile], axis=0)
            plane_copy(SWEEPS + 1, side).start()
        for side in range(2):
            plane_copy(SWEEPS + 1, side).wait_recv()
        far = pick(plane_mat[...], in_plane[SWEEPS + 1, :, 0].reshape(32, LANES))
        all_of(in_small, CORRECTION, recv_small)
        near = pick(lift_mat[...], in_small[CORRECTION].reshape(wide, LANES))
        for c in range(3):
            mine = jnp.broadcast_to(own[c], (8, LANES))

            def difference(values, start):
                return mine - jnp.broadcast_to(values[start : start + 8, c : c + 1], (8, LANES))

            gap = [difference(near, 8 * d) for d in range(4)]
            gap_lower, gap_upper = difference(far, 0), difference(far, 16)
            gap_k = jnp.where(first_k, gap[0], gap[1])
            for i in range(EDGE):
                for v in range(2):
                    change = MASS_TERM * effective[:, part(i, v)] * mine
                    change = change + ghost_k[:, part(i, v)] * gap_k
                    change = change + ghost_j[:, part(i, v)] * gap[2 + v]
                    if i == 0:
                        change = change + weight_i[:, part(0, v)] * gap_lower
                    if i == EDGE - 1:
                        change = change + weight_i[:, part(EDGE, v)] * gap_upper
                    residual[c, :, part(i, v)] = residual[c, :, part(i, v)] - change
                    velocity[c, :, part(i, v)] = velocity[c, :, part(i, v)] + mine

    def sweep(t, carry):
        @pl.when(t == DEG)
        def _():
            coarse_level()

        step = lax.rem(t, DEG)
        keep = by_step(step, [first for first, _ in steps])
        gain = by_step(step, [second for _, second in steps])

        @pl.loop(0, 3)
        def _(c):
            for i in range(EDGE):
                for v in range(2):
                    step_dir[c, :, part(i, v)] = keep * step_dir[c, :, part(i, v)] + gain * (
                        residual[c, :, part(i, v)] * inverse[:, part(i, v)]
                    )
            found = extract(lambda i, v: step_dir[c, :, part(i, v)])
            for (v, d), register in found.items():
                faces[c, pl.ds(v * 32 + d * 8, 8), :] = register

        packed = pick(pack_mat[...], side_by_side(lambda c: faces[c], 3))
        for c in range(3):
            out_big[t, :, c] = packed[:, c * LANES : (c + 1) * LANES].reshape(n_mem, 8, LANES)
        send(out_big, in_big, t, send_big, recv_big)
        send_planes(t, 3, lambda c, i, v: step_dir[c, :, part(i, v)])
        in_big[t, mem] = out_big[t, mem]

        @pl.loop(0, 3)
        def _(c):
            for i in range(EDGE):
                own = [step_dir[c, :, part(i, v)] for v in range(2)]
                back = [turn(x, EDGE) for x in own]
                ahead = [turn(x, -EDGE) for x in own]
                for v in range(2):
                    x = own[v]
                    if v == 0:
                        lower_j, upper_j = back[0], jnp.where(last_row, ahead[1], ahead[0])
                    else:
                        lower_j, upper_j = jnp.where(first_row, back[0], back[1]), ahead[1]
                    change = weight_k[0, :, part(i, v)] * turn(x, 1)
                    change = change + weight_k[1, :, part(i, v)] * turn(x, -1)
                    change = change + weight_j[0, :, part(i, v)] * lower_j
                    change = change + weight_j[1, :, part(i, v)] * upper_j
                    if i > 0:
                        change = change + weight_i[:, part(i, v)] * step_dir[c, :, part(i - 1, v)]
                    if i < EDGE - 1:
                        change = change + weight_i[:, part(i + 1, v)] * step_dir[
                            c, :, part(i + 1, v)
                        ]
                    residual[c, :, part(i, v)] = residual[c, :, part(i, v)] - (
                        diagonal[:, part(i, v)] * x - change
                    )
                    velocity[c, :, part(i, v)] = velocity[c, :, part(i, v)] + x

        receive_planes(t, 3)
        for c in range(3):
            for v in range(2):
                for i, side in ((0, 0), (EDGE - 1, 1)):
                    residual[c, :, part(i, v)] = residual[c, :, part(i, v)] + weight_i[
                        :, part(i + side, v)
                    ] * plane_ghost(c, side, v)
        all_of(in_big, t, recv_big)
        unpack_near(side_by_side(lambda c: in_big[t, :, c].reshape(wide, LANES), 3), 3)

        @pl.loop(0, 3)
        def _(c):
            for i in range(EDGE):
                for v in range(2):
                    change = ghost_k[:, part(i, v)] * k_ghost(c, i, v)
                    change = change + ghost_j[:, part(i, v)] * j_ghost(c, i, v)
                    residual[c, :, part(i, v)] = residual[c, :, part(i, v)] + change

        return carry

    lax.fori_loop(0, SWEEPS, sweep, 0)

    for t in range(SWEEPS + 1):
        all_of(out_big, t, send_big)
    for t in range(3):
        all_of(out_small, t, send_small)
    for t in range(SWEEPS + 2):
        for side in range(2):
            plane_copy(t, side).wait_send()


def solution(mesh):
    n_grp, n_mem = mesh.shape["grp"], mesh.shape["mem"]
    wide = n_mem * 8

    def local(*args):
        field = pltpu.VMEM((8, CELLS), F32)
        vmem = pl.BlockSpec(memory_space=pltpu.VMEM)
        smem = pl.BlockSpec(memory_space=pltpu.SMEM)
        forcing = args[0]
        dma = pltpu.SemaphoreType.DMA
        return pl.pallas_call(
            functools.partial(kernel, n_grp, n_mem),
            out_shape=[jax.ShapeDtypeStruct(forcing.shape, F32)] * 2,
            in_specs=[vmem, vmem, smem, vmem, vmem, vmem, vmem, vmem],
            out_specs=[vmem, vmem],
            scratch_shapes=[
                field,
                pltpu.VMEM((2, 8, CELLS), F32),
                pltpu.VMEM((2, 8, CELLS), F32),
                pltpu.VMEM((8, CELLS + FACE), F32),
                field,
                field,
                field,
                field,
                pltpu.VMEM((3, 8, CELLS), F32),
                pltpu.VMEM((3, 64, LANES), F32),
                pltpu.VMEM((3, 64, LANES), F32),
                pltpu.VMEM((3, 32, LANES), F32),
                pltpu.VMEM((32, LANES), F32),
                pltpu.VMEM((32, LANES), F32),
                pltpu.VMEM((64, wide), BF16),
                pltpu.VMEM((wide, 64), BF16),
                pltpu.VMEM((32, 32), BF16),
                pltpu.VMEM((32, wide), BF16),
                pltpu.VMEM((24, -(-n_mem * 24 // LANES) * LANES), F32),
                pltpu.VMEM((SWEEPS + 1, n_mem, 3, 8, LANES), F32),
                pltpu.VMEM((SWEEPS + 1, n_mem, 3, 8, LANES), F32),
                pltpu.VMEM((3, n_mem, 8, LANES), F32),
                pltpu.VMEM((3, n_mem, 8, LANES), F32),
                pltpu.VMEM((SWEEPS + 2, 2, 3, 16, LANES), F32),
                pltpu.VMEM((SWEEPS + 2, 2, 3, 16, LANES), F32),
                dma((SWEEPS + 1,)),
                dma((SWEEPS + 1,)),
                dma((3,)),
                dma((3,)),
                dma((SWEEPS + 2, 2)),
                dma((SWEEPS + 2, 2)),
            ],
            compiler_params=pltpu.CompilerParams(
                collective_id=0, has_side_effects=True, vmem_limit_bytes=32 * 1024 * 1024
            ),
            name="vcycle",
        )(*args)

    in_specs = (
        P(None, ("grp", "mem"), None),
        P(("grp", "mem"), None),
        P(("grp", "mem")),
        P(("grp", "mem"), None),
        P(("grp", "mem"), None),
        P(("grp", "mem"), None),
        P(("grp", "mem"), None),
        P("grp", "mem", None),
    )
    out_specs = (P(None, ("grp", "mem"), None), P(None, ("grp", "mem"), None))
    return jax.shard_map(local, mesh=mesh, in_specs=in_specs, out_specs=out_specs, check_vma=False)
```

time: 621 us -> 76.7 us (0.12); the launches traced: 609 us -> 76.1 us
  local copies, waits for them, and re-layouts: 207 us -> 6.27 us
  waiting for transfers between devices: 162 us -> 0 us
  other arithmetic: 92.3 us -> 0 us
  Pallas kernels: 0 us -> 69.1 us
  blocking collectives: 62.9 us -> 0 us
  matrix products: 41.7 us -> 0 us
  starting transfers between devices: 23.6 us -> 0 us
  between operations: 19.2 us -> 0.65 us
    all_gather x7 -> x0, waiting for transfers between devices: 160 us -> none  [near_faces(): gathered = lax.all_gather(face_rows, 'mem', axis=0, tiled=True)]
    reshape x95 -> x0, local copies, waits for them, and re-layouts: 74 us -> none  [the longest x42 35.4 us: coarsen(): return jnp.broadcast_to(average, squares.shape).reshape(leading + (FACE,))]
    pallas_call x0 -> x1, Pallas kernels: none -> 69.1 us  [local(): pl.pallas_call(functools.partial(kernel, n_grp, n_mem), out_shape=[jax.Sh...]
    reduce_sum x48 -> x0, other arithmetic: 42 us -> none  [coarsen(): average = jnp.mean(squares, axis=(-3, -1), keepdims=True)]
    dot_general x49 -> x0, matrix products: 41.7 us -> none  [the longest x32 27.8 us: beside(): jnp.einsum('cbim,lm->cbil', ghosts[direction].reshape(channels, blocks_he...]
    unnamed x1 -> x0, blocking collectives: 38.1 us -> none
    transpose x43 -> x0, local copies, waits for them, and re-layouts: 37.2 us -> none  [the longest x35 31.4 us: ghost_set(): ghost_rows[:, direction].transpose(1, 0, 2)]
    gather x24 -> x0, local copies, waits for them, and re-layouts: 30.1 us -> none  [the longest x8 16.5 us: near_faces(): return gathered[owners * (4 * blocks_here) + wanted]]
  transfers between devices with their start and end apart: 23 -> 0, of which waited for: 9 -> 0; matrix products, arithmetic and copies ran while one was open for 20% -> 0% of each run, Pallas kernels for 0% -> 0%
where the time goes in v1:
time: 76.7 us; the launch traced here: 76.1 us
  Pallas kernels  69.1 us (90%)
  local copies, waits for them, and re-layouts  6.27 us (8%)
    pallas_call x1, Pallas kernels, local(): pl.pallas_call(functools.partial(kernel, n_grp, n_mem), out_shape=[jax.Sh...  69.1 us
    unnamed x19, local copies, waits for them, and re-layouts  6.27 us

profile of v1, /device:TPU:0, one launch (start us, length us, event | category | flops | bytes accessed | tf_op | source)
XLA Modules:
  0.0 76.1 jit_solution(3073752686413316487)
XLA Ops:
  0.6 0.0 copy-start.5
  0.6 0.8 %copy.11.face_block = s32[8,4]{1,0:T(8,128)S(1)} copy(s32[8,4]{0,1:T(4,128)} %param.12) | data formatting | bytes 256 | tf_op args[4]
  1.4 0.0 copy-done.5
  1.4 0.0 copy-start.6
  1.4 0.1 copy.12.plane_block
  1.5 0.6 copy-done.6
  2.1 0.0 copy-start.3
  2.1 0.0 copy-start.4
  2.1 0.1 copy.10.face_owner
  2.2 0.6 copy-done.3
  2.7 0.0 copy-done.4
  2.8 0.0 copy-start
  2.8 1.0 %copy-done = f32[3,8,4096]{2,1,0:T(8,128)S(1)} copy-done((f32[3,8,4096]{2,1,0:T(8,128)S(1)}, f32[3,8,4096]{2,1,0:T(8,128)}, u32[]{:S(2)}) %copy-start) | copy-done | bytes 393240
  3.7 0.0 copy-start.1
  3.8 0.9 %copy-done.1 = f32[8,4096]{1,0:T(8,128)S(1)} copy-done((f32[8,4096]{1,0:T(8,128)S(1)}, f32[8,4096]{1,0:T(8,128)}, u32[]{:S(2)}) %copy-start.1) | copy-done | bytes 131096
  4.7 0.0 copy-start.2
  4.7 0.8 %copy-done.2 = f32[1,24,384]{2,1,0:T(8,128)S(1)} copy-done((f32[1,24,384]{2,1,0:T(8,128)S(1)}, f32[1,24,384]{2,1,0:T(8,128)}, u32[]{:S(2)}) %copy-start.2) | copy-done | bytes 36888
  5.4 69.1 %vcycle.1 = (f32[3,8,4096]{2,1,0:T(8,128)S(1)}, f32[3,8,4096]{2,1,0:T(8,128)S(1)}) custom-call(f32[3,8,4096]{2,1,0:T(8,128)S(1)} %copy-done, f32[8,4096]{1,0:T(8,128)S(1)} %copy-done.1, s32[8]{0:T(128)S(1)} %copy-done.4, s32[32,1]{1,0:T(8,128)S(1)} %copy.10.face_owner, s32[8,4]{1,0:T(8,128)S(1)} %copy.11.face_block, s32[8,2]{1,0:T(8,128)S(1)} %copy.12.plane_block, ...), custom_call_target="tpu_custom_call" | custom-call | tf_op jit(solution)/shard_map/vcycle/pallas_call | solution.py:550
  74.6 0.7 copy.15
  75.3 0.7 copy.16
Async XLA Ops:
  0.6 0.8 %copy-start.5 = (s32[8,2]{0,1:T(2,128)S(1)}, s32[8,2]{0,1:T(2,128)}, u32[]{:S(2)}) copy-start(s32[8,2]{0,1:T(2,128)} %param.13) | copy-start | bytes 196
  1.4 0.7 copy-start.6
  2.1 0.7 copy-start.3
  2.1 0.7 copy-start.4
  2.8 1.0 %copy-start = (f32[3,8,4096]{2,1,0:T(8,128)S(1)}, f32[3,8,4096]{2,1,0:T(8,128)}, u32[]{:S(2)}) copy-start(f32[3,8,4096]{2,1,0:T(8,128)} %forcing.1) | copy-start | bytes 1179652
  3.7 0.9 %copy-start.1 = (f32[8,4096]{1,0:T(8,128)S(1)}, f32[8,4096]{1,0:T(8,128)}, u32[]{:S(2)}) copy-start(f32[8,4096]{1,0:T(8,128)} %viscosity.1) | copy-start | bytes 393220
  4.7 0.8 %copy-start.2 = (f32[1,24,384]{2,1,0:T(8,128)S(1)}, f32[1,24,384]{2,1,0:T(8,128)}, u32[]{:S(2)}) copy-start(f32[1,24,384]{2,1,0:T(8,128)} %coarse_solver.1) | copy-start | bytes 110596

commit v2 on v1

--- a/solution.py
+++ b/solution.py
@@ -21,7 +21,7 @@
 SWEEPS = 2 * DEG
 F32 = jnp.float32
 BF16 = jnp.bfloat16
-REQUEST, EFFECTIVE, CORRECTION = 0, 1, 2
+REQUEST, CORRECTION = 0, 1
 
 
 def chebyshev():
@@ -37,6 +37,17 @@
     return steps
 
 
+def far_first(members):
+    tall = members // 4
+
+    def hops(offset):
+        dy, dx = offset
+        return min(dy, tall - dy) + min(dx, 4 - dx)
+
+    others = [(dy, dx) for dy in range(tall) for dx in range(4) if (dy, dx) != (0, 0)]
+    return sorted(others, key=hops, reverse=True)
+
+
 def by_step(step, values):
     result = jnp.float32(values[-1])
     for place in range(len(values) - 2, -1, -1):
@@ -57,16 +68,20 @@
     return pl.ds(i * FACE + v * LANES, LANES)
 
 
-def pick(one_hot, values):
+def parts(values):
     high = values.astype(BF16)
     rest = values - high.astype(F32)
     middle = rest.astype(BF16)
     low = (rest - middle.astype(F32)).astype(BF16)
-
-    def product(piece):
-        return jnp.dot(one_hot, piece, preferred_element_type=F32)
-
-    return product(high) + (product(middle) + product(low))
+    return jnp.concatenate([high, middle, low], axis=0)
+
+
+def thrice(one_hot):
+    return jnp.concatenate([one_hot] * 3, axis=1)
+
+
+def pick(one_hot_thrice, values):
+    return jnp.dot(one_hot_thrice, parts(values), preferred_element_type=F32)
 
 
 def coarsen(x):
@@ -102,19 +117,26 @@
     rows, columns = iota((32, 32), 0), iota((32, 32), 1)
     given = 4 * (rows % 8) + rows // 8
     given_t = 4 * (columns % 8) + columns // 8
-    across = jnp.sum(jnp.where(rows == columns, owner, 0), axis=0, keepdims=True)
-    owner_col = jnp.sum(jnp.where(columns == given, across, 0), axis=1, keepdims=True)
-    owner_row = jnp.sum(jnp.where(rows == given_t, owner, 0), axis=0, keepdims=True)
+    owner_col = jnp.sum(jnp.where(columns == given, owner, 0), axis=1, keepdims=True)
+    own_col = jnp.sum(jnp.where(rows == columns, owner, 0), axis=1, keepdims=True)
+    owner_row = jnp.sum(jnp.where(rows == given_t, own_col, 0), axis=0, keepdims=True)
     same = owner_col == owner_row
     rank_col = jnp.sum(jnp.where(same & (columns < rows), 1, 0), axis=1, keepdims=True)
     rank_row = jnp.sum(jnp.where(same & (rows < columns), 1, 0), axis=0, keepdims=True)
 
-    def spread(table, first, groups, of_row):
-        tall = jnp.concatenate([table] * groups, axis=0)
+    def spread(table, first, of_row):
+        tall = jnp.concatenate([table] * 4, axis=0)
         mask = iota(tall.shape, 1) == first + of_row(iota(tall.shape, 0))
         return jnp.sum(jnp.where(mask, tall, 0), axis=1, keepdims=True)
 
-    block_col = spread(face_block, 0, 4, lambda r: r // 8)
+    def spread_t(table, per):
+        lanes, which = iota((32, 8), 1), iota((32, 8), 0)
+        tall = jnp.zeros((32, 8), jnp.int32)
+        for d in range(table.shape[0]):
+            tall = jnp.where(which // per == d, table[d : d + 1], tall)
+        return jnp.sum(jnp.where(lanes == which % 8, tall, 0), axis=1, keepdims=True)
+
+    block_col = spread_t(face_block, 8)
     side = iota((32, 1), 0) // 8
     wanted = (side + 1 - 2 * (side % 2)) * 8 + block_col
     slot_col = owner_col * 8 + rank_col
@@ -128,34 +150,46 @@
     slots = iota((wide, 32), 0)
     unpack_t = jnp.concatenate([ones(slots == slot_row + CAP * v) for v in range(2)], axis=1)
     lanes = iota((32, LANES), 1)
-    source = jnp.concatenate([ones(lanes == wanted + 32 * v) for v in range(2)], axis=0)
+    source = jnp.concatenate([ones(lanes % 64 == wanted + 32 * v) for v in range(2)], axis=0)
     request = jnp.dot(unpack_t, source, preferred_element_type=F32)
-    plane_col = spread(plane_block, 0, 4, lambda r: r // 16)
+    lanes = iota((32, members * 64), 1)
+    face_pick = jnp.concatenate(
+        [ones(lanes == owner_col * 64 + wanted + 32 * v) for v in range(2)], axis=0
+    )
+    plane_col = spread_t(plane_block, 16)
     which = iota((32, 32), 0) // 16
     inside = jnp.where(which == 0, has_lower, has_upper) == 1
     plane_pick = ones((columns == rows // 8 * 8 + plane_col) & inside)
     lift_pick = ones(iota((32, wide), 1) == owner_col * 8 + block_col)
-    near_hang = spread(hanging, 0, 4, lambda r: r // 8)
-    plane_hang = spread(hanging, 4, 4, lambda r: r // 16)
+    near_hang = spread(hanging, 0, lambda r: r // 8)
+    plane_hang = spread(hanging, 4, lambda r: r // 16)
     near_hang = jnp.broadcast_to(near_hang.astype(F32), (32, LANES))
     plane_hang = jnp.broadcast_to(plane_hang.astype(F32), (32, LANES))
-    return unpack, request, plane_pick, lift_pick, near_hang, plane_hang
+    return (
+        thrice(unpack),
+        request,
+        thrice(face_pick),
+        thrice(plane_pick),
+        thrice(lift_pick),
+        near_hang,
+        plane_hang,
+    )
 
 
 def kernel(
     n_grp,
     n_mem,
-    forcing,
-    viscosity,
+    forcing_hbm,
+    viscosity_hbm,
+    solver_hbm,
     refinement,
     face_owner,
     face_block,
     plane_block,
     hanging,
-    coarse_solver,
-    velocity,
-    residual,
+    result,
     effective,
+    solver,
     weight_k,
     weight_j,
     weight_i,
@@ -173,7 +207,10 @@
     pack_mat,
     plane_mat,
     lift_mat,
+    face_mat,
     solver_rows,
+    out_face,
+    in_face,
     out_big,
     in_big,
     out_small,
@@ -186,7 +223,11 @@
     recv_small,
     send_plane,
     recv_plane,
+    send_face,
+    recv_face,
+    load_sem,
 ):
+    velocity, residual = result.at[0], result.at[1]
     grp, mem = lax.axis_index("grp"), lax.axis_index("mem")
     above = lax.rem(grp + 1, n_grp)
     below = lax.rem(grp + n_grp - 1, n_grp)
@@ -195,22 +236,32 @@
     wide = n_mem * 8
     COARSE = SWEEPS
 
+    mem_y, mem_x = lax.div(mem, 4), lax.rem(mem, 4)
+    peers = [
+        lax.rem(mem_y + dy, n_mem // 4) * 4 + lax.rem(mem_x + dx, 4) for dy, dx in far_first(n_mem)
+    ]
     barrier = pltpu.get_barrier_semaphore()
-    for offset in range(1, n_mem):
-        pl.semaphore_signal(
-            barrier, inc=1, device_id={"mem": lax.rem(mem + offset, n_mem)}, device_id_type=MESH
-        )
+    for to in peers:
+        pl.semaphore_signal(barrier, inc=1, device_id={"mem": to}, device_id_type=MESH)
     for other in (above, below):
         pl.semaphore_signal(barrier, inc=1, device_id={"grp": other}, device_id_type=MESH)
 
+    loads = [
+        pltpu.make_async_copy(viscosity_hbm, effective, load_sem.at[0]),
+        pltpu.make_async_copy(forcing_hbm, residual, load_sem.at[1]),
+        pltpu.make_async_copy(solver_hbm.at[0], solver, load_sem.at[2]),
+    ]
+    for load in loads:
+        load.start()
+
     lane = iota((8, LANES), 1)
     in_row = lane % EDGE
+    row = lane // EDGE
     first_k, last_k = in_row == 0, in_row == EDGE - 1
     first_row, last_row = lane < EDGE, lane >= LANES - EDGE
 
     def send(outgoing, incoming, which, send_sem, recv_sem):
-        for offset in range(1, n_mem):
-            to = lax.rem(mem + offset, n_mem)
+        for to in peers:
             pltpu.make_async_remote_copy(
                 src_ref=outgoing.at[which, to],
                 dst_ref=incoming.at[which, mem],
@@ -234,7 +285,7 @@
             device_id_type=MESH,
         )
 
-    unpack, request, plane_pick, lift_pick, near_hang, plane_hang = tables(
+    unpack, request, face_pick, plane_pick, lift_pick, near_hang, plane_hang = tables(
         face_owner[...],
         face_block[...],
         plane_block[...],
@@ -244,25 +295,23 @@
         jnp.where(grp < n_grp - 1, 1, 0),
     )
     unpack_mat[...] = unpack
+    face_mat[...] = face_pick
     plane_mat[...] = plane_pick
     lift_mat[...] = lift_pick
     hang_near[...] = near_hang
     hang_plane[...] = plane_hang
     out_small[REQUEST] = request.reshape(n_mem, 8, LANES)
 
-    pl.semaphore_wait(barrier, n_mem - 1 + 2)
-
-    send(out_small, in_small, REQUEST, send_small, recv_small)
-    in_small[REQUEST, mem] = out_small[REQUEST, mem]
-
     block_row = iota((8, LANES), 0)
-    level = jnp.zeros((8, LANES), jnp.int32)
-    for b in range(8):
-        level = jnp.where(block_row == b, refinement[b], level)
+    level = jnp.sum(
+        jnp.where(iota((8, 8), 0) == iota((8, 8), 1), refinement[...], 0), axis=1, keepdims=True
+    )
+    level = jnp.broadcast_to(level, (8, LANES))
     scale = 1.0 / jnp.left_shift(jnp.ones_like(level), level).astype(F32)
+    loads[0].wait()
     for i in range(EDGE):
         for v in range(2):
-            effective[:, part(i, v)] = viscosity[:, part(i, v)] * scale
+            effective[:, part(i, v)] = effective[:, part(i, v)] * scale
 
     def send_planes(which, channels, read):
         for c in range(channels):
@@ -275,27 +324,37 @@
     for side in range(2):
         for c in range(1, 3):
             out_plane[SWEEPS, side, c] = jnp.zeros((16, LANES), F32)
-    send_planes(SWEEPS, 1, lambda c, i, v: effective[:, part(i, v)])
     found = extract(lambda i, v: effective[:, part(i, v)])
     for (v, d), register in found.items():
-        faces[0, pl.ds(v * 32 + d * 8, 8), :] = register
-
-    all_of(in_small, REQUEST, recv_small)
-    pack_mat[...] = in_small[REQUEST].reshape(wide, LANES)[:, :64].astype(BF16)
-    out_small[EFFECTIVE] = pick(pack_mat[...], faces[0]).reshape(n_mem, 8, LANES)
-    send(out_small, in_small, EFFECTIVE, send_small, recv_small)
-    in_small[EFFECTIVE, mem] = out_small[EFFECTIVE, mem]
-
+        out_face[pl.ds(v * 32 + d * 8, 8), :] = register
+
+    pl.semaphore_wait(barrier, n_mem - 1 + 2)
+
+    for to in peers:
+        pltpu.make_async_remote_copy(
+            src_ref=out_face,
+            dst_ref=in_face.at[mem],
+            send_sem=send_face,
+            recv_sem=recv_face,
+            device_id={"mem": to},
+            device_id_type=MESH,
+        ).start()
+    send_planes(SWEEPS, 1, lambda c, i, v: effective[:, part(i, v)])
+    send(out_small, in_small, REQUEST, send_small, recv_small)
+    in_face[mem] = out_face[...]
+    in_small[REQUEST, mem] = out_small[REQUEST, mem]
+
+    loads[1].wait()
+    loads[2].wait()
     rows, columns = iota((24, 24), 0), iota((24, 24), 1)
     reorder = jnp.where(columns == 3 * (rows % 8) + rows // 8, 1.0, 0.0).astype(BF16)
-    solver_rows[:, pl.ds(0, n_coarse)] = pick(reorder, coarse_solver[0])
+    solver_rows[:, pl.ds(0, n_coarse)] = pick(thrice(reorder), solver[...])
     if n_coarse % LANES:
         spare = groups_of_lanes * LANES - n_coarse
         solver_rows[:, pl.ds(n_coarse, spare)] = jnp.zeros((24, spare), F32)
     for c in range(3):
         for i in range(EDGE):
             for v in range(2):
-                residual[c, :, part(i, v)] = forcing[c, :, part(i, v)]
                 velocity[c, :, part(i, v)] = jnp.zeros((8, LANES), F32)
                 step_dir[c, :, part(i, v)] = jnp.zeros((8, LANES), F32)
     for i in range(EDGE):
@@ -336,8 +395,8 @@
         for c in range(channels):
             plane_ghosts[c] = settle(picked[:, c * LANES : (c + 1) * LANES], hang_plane[...])
 
-    def unpack_near(arrived, channels):
-        picked = pick(unpack_mat[...], arrived)
+    def unpack_near(matrix, arrived, channels):
+        picked = pick(matrix, arrived)
         for c in range(channels):
             for v in range(2):
                 ghosts[c, pl.ds(32 * v, 32), :] = settle(
@@ -350,27 +409,36 @@
     def plane_ghost(c, side, v):
         return plane_ghosts[c, pl.ds(side * 16 + v * 8, 8), :]
 
-    def k_ghost(c, i, v):
-        return jnp.where(first_k, turn(ghost(c, 0, v), -i), turn(ghost(c, 1, v), EDGE - 1 - i))
-
-    def j_ghost(c, i, v):
-        shift = -(i % 8) * EDGE
-        if v == 0:
-            return turn(ghost(c, 2, i // 8), shift)
-        return turn(ghost(c, 3, i // 8), LANES - EDGE + shift)
+    def near_ghosts(c):
+        lower_k = [ghost(c, 0, v) for v in range(2)]
+        upper_k = [turn(ghost(c, 1, v), EDGE - 1) for v in range(2)]
+        lower_j = [ghost(c, 2, v) for v in range(2)]
+        upper_j = [turn(ghost(c, 3, v), LANES - EDGE) for v in range(2)]
+
+        def at_k(i, v):
+            return turn(jnp.where(in_row == i, lower_k[v], upper_k[v]), -i)
+
+        def at_j(i):
+            both = jnp.where(row == i % 8, lower_j[i // 8], upper_j[i // 8])
+            return turn(both, -(i % 8) * EDGE)
+
+        return at_k, at_j
 
     receive_planes(SWEEPS, 1)
     for v in range(2):
         weight_i[:, part(0, v)] = 0.5 * (effective[:, part(0, v)] + plane_ghost(0, 0, v))
         weight_i[:, part(EDGE, v)] = 0.5 * (effective[:, part(EDGE - 1, v)] + plane_ghost(0, 1, v))
-    all_of(in_small, EFFECTIVE, recv_small)
-    unpack_near(in_small[EFFECTIVE].reshape(wide, LANES), 1)
+    span = in_face.at[pl.ds(0, n_mem - 1)]
+    pltpu.make_async_copy(span, span, recv_face).wait()
+    unpack_near(face_mat[...], in_face[...].reshape(n_mem * 64, LANES), 1)
+    k_ghost, j_ghost = near_ghosts(0)
     for i in range(EDGE):
+        beside_j = j_ghost(i)
         for v in range(2):
             x = effective[:, part(i, v)]
-            at_k = jnp.where(first_k | last_k, 0.5 * (x + k_ghost(0, i, v)), 0.0)
+            at_k = jnp.where(first_k | last_k, 0.5 * (x + k_ghost(i, v)), 0.0)
             edge = first_row if v == 0 else last_row
-            at_j = jnp.where(edge, 0.5 * (x + j_ghost(0, i, v)), 0.0)
+            at_j = jnp.where(edge, 0.5 * (x + beside_j), 0.0)
             ghost_k[:, part(i, v)] = at_k
             ghost_j[:, part(i, v)] = at_j
             whole = (
@@ -382,14 +450,39 @@
             inverse[:, part(i, v)] = 1.0 / whole
 
     steps = chebyshev()
+    ghosts[...] = jnp.zeros(ghosts.shape, F32)
+    plane_ghosts[...] = jnp.zeros(plane_ghosts.shape, F32)
+    all_of(in_small, REQUEST, recv_small)
+    request = in_small[REQUEST].reshape(wide, LANES)
+    pack_mat[...] = jnp.concatenate([request, request[:, :64]], axis=1).astype(BF16)
+
+    def across_faces(c):
+        k_ghost, j_ghost = near_ghosts(c)
+
+        def new(i):
+            beside_j = j_ghost(i)
+            result = []
+            for v in range(2):
+                change = ghost_k[:, part(i, v)] * k_ghost(i, v)
+                change = change + ghost_j[:, part(i, v)] * beside_j
+                if i == 0:
+                    change = change + weight_i[:, part(0, v)] * plane_ghost(c, 0, v)
+                if i == EDGE - 1:
+                    change = change + weight_i[:, part(EDGE, v)] * plane_ghost(c, 1, v)
+                result.append(residual[c, :, part(i, v)] + change)
+            return result
+
+        return new
 
     def coarse_level():
         totals = []
         for c in range(3):
             total = jnp.zeros((8, LANES), F32)
+            new = across_faces(c)
             for i in range(EDGE):
-                for v in range(2):
-                    total = total + residual[c, :, part(i, v)]
+                for v, value in enumerate(new(i)):
+                    residual[c, :, part(i, v)] = value
+                    total = total + value
             totals.append(jnp.sum(total, axis=1, keepdims=True) / math.sqrt(CELLS))
         for q in range(groups_of_lanes):
             place = lane + q * LANES - 24 * mem - 3 * block_row
@@ -451,6 +544,8 @@
                         change = change + weight_i[:, part(EDGE, v)] * gap_upper
                     residual[c, :, part(i, v)] = residual[c, :, part(i, v)] - change
                     velocity[c, :, part(i, v)] = velocity[c, :, part(i, v)] + mine
+        ghosts[...] = jnp.zeros(ghosts.shape, F32)
+        plane_ghosts[...] = jnp.zeros(plane_ghosts.shape, F32)
 
     def sweep(t, carry):
         @pl.when(t == DEG)
@@ -461,15 +556,22 @@
         keep = by_step(step, [first for first, _ in steps])
         gain = by_step(step, [second for _, second in steps])
 
-        @pl.loop(0, 3)
-        def _(c):
-            for i in range(EDGE):
-                for v in range(2):
-                    step_dir[c, :, part(i, v)] = keep * step_dir[c, :, part(i, v)] + gain * (
-                        residual[c, :, part(i, v)] * inverse[:, part(i, v)]
-                    )
-            found = extract(lambda i, v: step_dir[c, :, part(i, v)])
-            for (v, d), register in found.items():
+        for c in range(3):
+            new = across_faces(c)
+            moved = {}
+
+            def step_of(i, v):
+                if v == 0:
+                    for half, value in enumerate(new(i)):
+                        residual[c, :, part(i, half)] = value
+                        ahead = keep * step_dir[c, :, part(i, half)] + gain * (
+                            value * inverse[:, part(i, half)]
+                        )
+                        step_dir[c, :, part(i, half)] = ahead
+                        moved[i, half] = ahead
+                return moved[i, v]
+
+            for (v, d), register in extract(step_of).items():
                 faces[c, pl.ds(v * 32 + d * 8, 8), :] = register
 
         packed = pick(pack_mat[...], side_by_side(lambda c: faces[c], 3))
@@ -507,30 +609,26 @@
                     velocity[c, :, part(i, v)] = velocity[c, :, part(i, v)] + x
 
         receive_planes(t, 3)
-        for c in range(3):
-            for v in range(2):
-                for i, side in ((0, 0), (EDGE - 1, 1)):
-                    residual[c, :, part(i, v)] = residual[c, :, part(i, v)] + weight_i[
-                        :, part(i + side, v)
-                    ] * plane_ghost(c, side, v)
         all_of(in_big, t, recv_big)
-        unpack_near(side_by_side(lambda c: in_big[t, :, c].reshape(wide, LANES), 3), 3)
-
-        @pl.loop(0, 3)
-        def _(c):
-            for i in range(EDGE):
-                for v in range(2):
-                    change = ghost_k[:, part(i, v)] * k_ghost(c, i, v)
-                    change = change + ghost_j[:, part(i, v)] * j_ghost(c, i, v)
-                    residual[c, :, part(i, v)] = residual[c, :, part(i, v)] + change
-
+        unpack_near(
+            unpack_mat[...],
+            side_by_side(lambda c: in_big[t, :, c].reshape(wide, LANES), 3),
+            3,
+        )
         return carry
 
     lax.fori_loop(0, SWEEPS, sweep, 0)
-
+    for c in range(3):
+        new = across_faces(c)
+        for i in range(EDGE):
+            for v, value in enumerate(new(i)):
+                residual[c, :, part(i, v)] = value
+
+    span = in_face.at[pl.ds(0, n_mem - 1)]
+    pltpu.make_async_copy(span, span, send_face).wait()
     for t in range(SWEEPS + 1):
         all_of(out_big, t, send_big)
-    for t in range(3):
+    for t in (REQUEST, CORRECTION):
         all_of(out_small, t, send_small)
     for t in range(SWEEPS + 2):
         for side in range(2):
@@ -541,19 +639,28 @@
     n_grp, n_mem = mesh.shape["grp"], mesh.shape["mem"]
     wide = n_mem * 8
 
-    def local(*args):
+    def local(
+        forcing,
+        viscosity,
+        refinement,
+        face_owner,
+        face_block,
+        plane_block,
+        hanging,
+        coarse_solver,
+    ):
         field = pltpu.VMEM((8, CELLS), F32)
         vmem = pl.BlockSpec(memory_space=pltpu.VMEM)
-        smem = pl.BlockSpec(memory_space=pltpu.SMEM)
-        forcing = args[0]
+        hbm = pl.BlockSpec(memory_space=pltpu.HBM)
         dma = pltpu.SemaphoreType.DMA
-        return pl.pallas_call(
+        both = pl.pallas_call(
             functools.partial(kernel, n_grp, n_mem),
-            out_shape=[jax.ShapeDtypeStruct(forcing.shape, F32)] * 2,
-            in_specs=[vmem, vmem, smem, vmem, vmem, vmem, vmem, vmem],
-            out_specs=[vmem, vmem],
+            out_shape=jax.ShapeDtypeStruct((2, *forcing.shape), F32),
+            in_specs=[hbm] * 3 + [vmem] * 5,
+            out_specs=vmem,
             scratch_shapes=[
                 field,
+                pltpu.VMEM((24, n_mem * 24), F32),
                 pltpu.VMEM((2, 8, CELLS), F32),
                 pltpu.VMEM((2, 8, CELLS), F32),
                 pltpu.VMEM((8, CELLS + FACE), F32),
@@ -567,29 +674,45 @@
                 pltpu.VMEM((3, 32, LANES), F32),
                 pltpu.VMEM((32, LANES), F32),
                 pltpu.VMEM((32, LANES), F32),
-                pltpu.VMEM((64, wide), BF16),
-                pltpu.VMEM((wide, 64), BF16),
-                pltpu.VMEM((32, 32), BF16),
-                pltpu.VMEM((32, wide), BF16),
+                pltpu.VMEM((64, 3 * wide), BF16),
+                pltpu.VMEM((wide, 192), BF16),
+                pltpu.VMEM((32, 96), BF16),
+                pltpu.VMEM((32, 3 * wide), BF16),
+                pltpu.VMEM((64, 3 * n_mem * 64), BF16),
                 pltpu.VMEM((24, -(-n_mem * 24 // LANES) * LANES), F32),
+                pltpu.VMEM((64, LANES), F32),
+                pltpu.VMEM((n_mem, 64, LANES), F32),
                 pltpu.VMEM((SWEEPS + 1, n_mem, 3, 8, LANES), F32),
                 pltpu.VMEM((SWEEPS + 1, n_mem, 3, 8, LANES), F32),
-                pltpu.VMEM((3, n_mem, 8, LANES), F32),
-                pltpu.VMEM((3, n_mem, 8, LANES), F32),
+                pltpu.VMEM((2, n_mem, 8, LANES), F32),
+                pltpu.VMEM((2, n_mem, 8, LANES), F32),
                 pltpu.VMEM((SWEEPS + 2, 2, 3, 16, LANES), F32),
                 pltpu.VMEM((SWEEPS + 2, 2, 3, 16, LANES), F32),
                 dma((SWEEPS + 1,)),
                 dma((SWEEPS + 1,)),
-                dma((3,)),
-                dma((3,)),
+                dma((2,)),
+                dma((2,)),
                 dma((SWEEPS + 2, 2)),
                 dma((SWEEPS + 2, 2)),
+                dma,
+                dma,
+                dma((3,)),
             ],
             compiler_params=pltpu.CompilerParams(
-                collective_id=0, has_side_effects=True, vmem_limit_bytes=32 * 1024 * 1024
+                collective_id=0, has_side_effects=True, vmem_limit_bytes=56 * 1024 * 1024
             ),
             name="vcycle",
-        )(*args)
+        )(
+            forcing,
+            viscosity,
+            coarse_solver,
+            refinement.reshape(1, 8),
+            face_owner.reshape(1, 32),
+            face_block.T,
+            plane_block.T,
+            hanging,
+        )
+        return both[0], both[1]
 
     in_specs = (
         P(None, ("grp", "mem"), None),

time: 76.7 us -> 67.2 us (0.88)
  Pallas kernels: 69.1 us -> 64 us
  local copies, waits for them, and re-layouts: 6.27 us -> 2.04 us
    unnamed x19 -> x0, local copies, waits for them, and re-layouts: 6.27 us -> none
    pallas_call x1, Pallas kernels: 69.1 us -> 64 us  [local(): pl.pallas_call(functools.partial(kernel, n_grp, n_mem), out_shape=jax.Sha...]
    squeeze x0 -> x1, local copies, waits for them, and re-layouts: none -> 2.04 us  [local(): return (both[0], both[1])]
where the time goes in v2:
time: 67.2 us; the launch traced here: 66.7 us
  Pallas kernels  64 us (95%)
  local copies, waits for them, and re-layouts  2.04 us (3%)
    pallas_call x1, Pallas kernels, local(): pl.pallas_call(functools.partial(kernel, n_grp, n_mem), out_shape=jax.Sha...  64 us
    squeeze x1, local copies, waits for them, and re-layouts, local(): return (both[0], both[1])  2.04 us

profile of v2, /device:TPU:0, one launch (start us, length us, event | category | flops | bytes accessed | tf_op | source)
XLA Modules:
  0.0 66.7 jit_solution(16504123813808588865)
XLA Ops:
  0.6 64.0 %vcycle.1 = f32[2,3,8,4096]{3,2,1,0:T(8,128)} custom-call(f32[3,8,4096]{2,1,0:T(8,128)} %forcing_hbm.1, f32[8,4096]{1,0:T(8,128)} %viscosity_hbm.1, f32[1,24,384]{2,1,0:T(8,128)} %solver_hbm.1, s32[1,8]{1,0:T(1,128)} %bitcast.10, s32[1,32]{1,0:T(1,128)} %bitcast.11, s32[4,8]{1,0:T(4,128)} %bitcast.8, s32[2,8]{1,0:T(2,128)} %bitcast.9, s32[8,6]{1,0:T(8,128)} %hanging.1), custom_call_target="tpu_custom_call" | custom-call | tf_op jit(solution)/shard_map/vcycle/pallas_call | solution.py:656
  64.7 2.0 %slice_bitcast_fusion = (f32[3,8,4096]{2,1,0:T(8,128)}, f32[3,8,4096]{2,1,0:T(8,128)}) fusion(f32[2,3,8,4096]{3,2,1,0:T(8,128)} %vcycle.1), kind=kLoop, calls=%fused_computation | loop fusion | bytes 1572864 | tf_op jit(solution)/shard_map/squeeze | solution.py:715

commit v3 on v2

--- a/solution.py
+++ b/solution.py
@@ -21,7 +21,6 @@
 SWEEPS = 2 * DEG
 F32 = jnp.float32
 BF16 = jnp.bfloat16
-REQUEST, CORRECTION = 0, 1
 
 
 def chebyshev():
@@ -152,14 +151,16 @@
     lanes = iota((32, LANES), 1)
     source = jnp.concatenate([ones(lanes % 64 == wanted + 32 * v) for v in range(2)], axis=0)
     request = jnp.dot(unpack_t, source, preferred_element_type=F32)
-    lanes = iota((32, members * 64), 1)
-    face_pick = jnp.concatenate(
-        [ones(lanes == owner_col * 64 + wanted + 32 * v) for v in range(2)], axis=0
-    )
     plane_col = spread_t(plane_block, 16)
     which = iota((32, 32), 0) // 16
     inside = jnp.where(which == 0, has_lower, has_upper) == 1
     plane_pick = ones((columns == rows // 8 * 8 + plane_col) & inside)
+    lanes, which = iota((8, 8), 1), iota((8, 8), 0)
+    far_pick = []
+    for d, exists in enumerate((has_lower, has_upper)):
+        chosen = plane_block[d : d + 1]
+        chosen = jnp.sum(jnp.where(lanes == which, chosen, 0), axis=1, keepdims=True)
+        far_pick.append(jnp.where((lanes == chosen) & (exists == 1), 1.0, 0.0))
     lift_pick = ones(iota((32, wide), 1) == owner_col * 8 + block_col)
     near_hang = spread(hanging, 0, lambda r: r // 8)
     plane_hang = spread(hanging, 4, lambda r: r // 16)
@@ -168,9 +169,9 @@
     return (
         thrice(unpack),
         request,
-        thrice(face_pick),
         thrice(plane_pick),
         thrice(lift_pick),
+        far_pick,
         near_hang,
         plane_hang,
     )
@@ -187,7 +188,11 @@
     face_block,
     plane_block,
     hanging,
+    owner_scalar,
+    block_scalar,
     result,
+    velocity,
+    residual,
     effective,
     solver,
     weight_k,
@@ -207,34 +212,45 @@
     pack_mat,
     plane_mat,
     lift_mat,
-    face_mat,
+    far_mat,
     solver_rows,
+    in_solver,
+    in_far_solver,
+    near_rows,
+    far_rows,
+    out_vector,
+    in_vector,
     out_face,
     in_face,
     out_big,
     in_big,
-    out_small,
-    in_small,
+    out_request,
+    in_request,
     out_plane,
     in_plane,
     send_big,
     recv_big,
-    send_small,
-    recv_small,
+    send_request,
+    recv_request,
     send_plane,
     recv_plane,
     send_face,
     recv_face,
+    send_solver,
+    recv_solver,
+    send_far,
+    recv_far,
+    send_vector,
+    recv_vector,
     load_sem,
+    store_sem,
 ):
-    velocity, residual = result.at[0], result.at[1]
     grp, mem = lax.axis_index("grp"), lax.axis_index("mem")
     above = lax.rem(grp + 1, n_grp)
     below = lax.rem(grp + n_grp - 1, n_grp)
     n_coarse = n_mem * 24
-    groups_of_lanes = -(-n_coarse // LANES)
+    groups_of_lanes = n_coarse // LANES
     wide = n_mem * 8
-    COARSE = SWEEPS
 
     mem_y, mem_x = lax.div(mem, 4), lax.rem(mem, 4)
     peers = [
@@ -244,7 +260,10 @@
     for to in peers:
         pl.semaphore_signal(barrier, inc=1, device_id={"mem": to}, device_id_type=MESH)
     for other in (above, below):
-        pl.semaphore_signal(barrier, inc=1, device_id={"grp": other}, device_id_type=MESH)
+        for to in [*peers, mem]:
+            pl.semaphore_signal(
+                barrier, inc=1, device_id={"grp": other, "mem": to}, device_id_type=MESH
+            )
 
     loads = [
         pltpu.make_async_copy(viscosity_hbm, effective, load_sem.at[0]),
@@ -254,26 +273,30 @@
     for load in loads:
         load.start()
 
+    def store(place):
+        source = (velocity, residual)[place]
+        return pltpu.make_async_copy(source, result.at[place], store_sem.at[place])
+
     lane = iota((8, LANES), 1)
     in_row = lane % EDGE
     row = lane // EDGE
     first_k, last_k = in_row == 0, in_row == EDGE - 1
     first_row, last_row = lane < EDGE, lane >= LANES - EDGE
 
-    def send(outgoing, incoming, which, send_sem, recv_sem):
+    def send(outgoing, incoming, send_sem, recv_sem):
         for to in peers:
             pltpu.make_async_remote_copy(
-                src_ref=outgoing.at[which, to],
-                dst_ref=incoming.at[which, mem],
-                send_sem=send_sem.at[which],
-                recv_sem=recv_sem.at[which],
+                src_ref=outgoing.at[to],
+                dst_ref=incoming.at[mem],
+                send_sem=send_sem,
+                recv_sem=recv_sem,
                 device_id={"mem": to},
                 device_id_type=MESH,
             ).start()
 
-    def all_of(buffer, which, sem):
-        span = buffer.at[which, pl.ds(0, n_mem - 1)]
-        pltpu.make_async_copy(span, span, sem.at[which]).wait()
+    def wait_for(buffer, sem, count=n_mem - 1):
+        span = buffer.at[pl.ds(0, count)]
+        pltpu.make_async_copy(span, span, sem).wait()
 
     def plane_copy(which, side):
         return pltpu.make_async_remote_copy(
@@ -285,22 +308,15 @@
             device_id_type=MESH,
         )
 
-    unpack, request, face_pick, plane_pick, lift_pick, near_hang, plane_hang = tables(
-        face_owner[...],
-        face_block[...],
-        plane_block[...],
-        hanging[...],
-        n_mem,
-        jnp.where(grp > 0, 1, 0),
-        jnp.where(grp < n_grp - 1, 1, 0),
-    )
-    unpack_mat[...] = unpack
-    face_mat[...] = face_pick
-    plane_mat[...] = plane_pick
-    lift_mat[...] = lift_pick
-    hang_near[...] = near_hang
-    hang_plane[...] = plane_hang
-    out_small[REQUEST] = request.reshape(n_mem, 8, LANES)
+    def far_solver(c, side):
+        return pltpu.make_async_remote_copy(
+            src_ref=solver_rows.at[c],
+            dst_ref=in_far_solver.at[c, side],
+            send_sem=send_far.at[c, side],
+            recv_sem=recv_far.at[c, side],
+            device_id={"grp": above if side == 0 else below},
+            device_id_type=MESH,
+        )
 
     block_row = iota((8, LANES), 0)
     level = jnp.sum(
@@ -328,7 +344,7 @@
     for (v, d), register in found.items():
         out_face[pl.ds(v * 32 + d * 8, 8), :] = register
 
-    pl.semaphore_wait(barrier, n_mem - 1 + 2)
+    pl.semaphore_wait(barrier, n_mem - 1 + 2 * n_mem)
 
     for to in peers:
         pltpu.make_async_remote_copy(
@@ -340,18 +356,34 @@
             device_id_type=MESH,
         ).start()
     send_planes(SWEEPS, 1, lambda c, i, v: effective[:, part(i, v)])
-    send(out_small, in_small, REQUEST, send_small, recv_small)
     in_face[mem] = out_face[...]
-    in_small[REQUEST, mem] = out_small[REQUEST, mem]
+    unpack, request, plane_pick, lift_pick, far_pick, near_hang, plane_hang = tables(
+        face_owner[...],
+        face_block[...],
+        plane_block[...],
+        hanging[...],
+        n_mem,
+        jnp.where(grp > 0, 1, 0),
+        jnp.where(grp < n_grp - 1, 1, 0),
+    )
+    unpack_mat[...] = unpack
+    plane_mat[...] = plane_pick
+    lift_mat[...] = lift_pick
+    for side in range(2):
+        far_mat[side] = far_pick[side]
+    hang_near[...] = near_hang
+    hang_plane[...] = plane_hang
+    out_request[...] = request.reshape(n_mem, 8, LANES)
+    send(out_request, in_request, send_request, recv_request)
+    in_request[mem] = out_request[mem]
 
     loads[1].wait()
     loads[2].wait()
     rows, columns = iota((24, 24), 0), iota((24, 24), 1)
     reorder = jnp.where(columns == 3 * (rows % 8) + rows // 8, 1.0, 0.0).astype(BF16)
-    solver_rows[:, pl.ds(0, n_coarse)] = pick(thrice(reorder), solver[...])
-    if n_coarse % LANES:
-        spare = groups_of_lanes * LANES - n_coarse
-        solver_rows[:, pl.ds(n_coarse, spare)] = jnp.zeros((24, spare), F32)
+    ordered = pick(thrice(reorder), solver[...])
+    for c in range(3):
+        solver_rows[c] = ordered[8 * c : 8 * c + 8]
     for c in range(3):
         for i in range(EDGE):
             for v in range(2):
@@ -428,9 +460,17 @@
     for v in range(2):
         weight_i[:, part(0, v)] = 0.5 * (effective[:, part(0, v)] + plane_ghost(0, 0, v))
         weight_i[:, part(EDGE, v)] = 0.5 * (effective[:, part(EDGE - 1, v)] + plane_ghost(0, 1, v))
-    span = in_face.at[pl.ds(0, n_mem - 1)]
-    pltpu.make_async_copy(span, span, recv_face).wait()
-    unpack_near(face_mat[...], in_face[...].reshape(n_mem * 64, LANES), 1)
+    wait_for(in_face, recv_face)
+    for d in range(4):
+        for b in range(8):
+            owner = owner_scalar[0, 4 * b + d]
+            wanted = (d + 1 - 2 * (d % 2)) * 8 + block_scalar[d, b]
+            for v in range(2):
+                ghosts[0, pl.ds(v * 32 + d * 8 + b, 1), :] = in_face[
+                    owner, pl.ds(v * 32 + wanted, 1), :
+                ]
+    for v in range(2):
+        ghosts[0, pl.ds(32 * v, 32), :] = settle(ghosts[0, pl.ds(32 * v, 32), :], hang_near[...])
     k_ghost, j_ghost = near_ghosts(0)
     for i in range(EDGE):
         beside_j = j_ghost(i)
@@ -452,8 +492,8 @@
     steps = chebyshev()
     ghosts[...] = jnp.zeros(ghosts.shape, F32)
     plane_ghosts[...] = jnp.zeros(plane_ghosts.shape, F32)
-    all_of(in_small, REQUEST, recv_small)
-    request = in_small[REQUEST].reshape(wide, LANES)
+    wait_for(in_request, recv_request)
+    request = in_request[...].reshape(wide, LANES)
     pack_mat[...] = jnp.concatenate([request, request[:, :64]], axis=1).astype(BF16)
 
     def across_faces(c):
@@ -484,54 +524,74 @@
                     residual[c, :, part(i, v)] = value
                     total = total + value
             totals.append(jnp.sum(total, axis=1, keepdims=True) / math.sqrt(CELLS))
+        chunks = []
         for q in range(groups_of_lanes):
             place = lane + q * LANES - 24 * mem - 3 * block_row
             mine = jnp.zeros((8, LANES), F32)
             for c in range(3):
                 mine = jnp.where(place == c, totals[c], mine)
-            for m in range(n_mem):
-                out_big[COARSE, m, q] = mine
-        for q in range(groups_of_lanes, 3):
-            for m in range(n_mem):
-                out_big[COARSE, m, q] = jnp.zeros((8, LANES), F32)
-        send(out_big, in_big, COARSE, send_big, recv_big)
-        in_big[COARSE, mem] = out_big[COARSE, mem]
-        all_of(in_big, COARSE, recv_big)
-        products = [jnp.zeros((8, LANES), F32)] * 3
+            chunks.append(jnp.sum(mine, axis=0, keepdims=True))
+        tile = jnp.zeros((8, LANES), F32)
         for q in range(groups_of_lanes):
-            vector = in_big[COARSE, 0, q]
+            tile = jnp.where(block_row == q, chunks[q], tile)
+        out_vector[...] = tile
+
+        def send_vector_to(other, to, slot):
+            pltpu.make_async_remote_copy(
+                src_ref=out_vector,
+                dst_ref=in_vector.at[slot, mem],
+                send_sem=send_vector.at[slot],
+                recv_sem=recv_vector.at[slot],
+                device_id={"grp": other, "mem": to},
+                device_id_type=MESH,
+            ).start()
+
+        for to in peers:
+            send_vector_to(above, to, 1)
+            send_vector_to(below, to, 2)
+            send_vector_to(grp, to, 0)
+        send_vector_to(above, mem, 1)
+        send_vector_to(below, mem, 2)
+        in_vector[0, mem] = tile
+
+        for c in range(3):
+            wait_for(in_solver.at[c], recv_solver.at[c])
+            in_solver[c, mem] = solver_rows[c]
+            near_rows[c] = pick(lift_mat[...], in_solver[c].reshape(wide, n_coarse))
+            for side in range(2):
+                far_solver(c, side).wait_recv()
+                source = in_far_solver[c, side]
+                chosen = jnp.zeros((8, n_coarse), F32)
+                for b in range(8):
+                    wants = far_mat[side][:, b : b + 1]
+                    chosen = jnp.where(wants == 1.0, source[b : b + 1], chosen)
+                far_rows[c, side] = chosen
+
+        def vector_of(slot):
+            whole = in_vector[slot, 0]
             for m in range(1, n_mem):
-                vector = vector + in_big[COARSE, m, q]
-            vector = jnp.sum(vector, axis=0, keepdims=True)
-            for c in range(3):
-                products[c] = products[c] + solver_rows[
-                    pl.ds(8 * c, 8), pl.ds(q * LANES, LANES)
-                ] * vector
-        own = [jnp.sum(products[c], axis=1, keepdims=True) for c in range(3)]
-        tile = jnp.zeros((8, LANES), F32)
+                whole = whole + in_vector[slot, m]
+            return [jnp.broadcast_to(whole[q : q + 1], (8, LANES)) for q in range(groups_of_lanes)]
+
+        def correction(rows, vector):
+            product = rows[:, :LANES] * vector[0]
+            for q in range(1, groups_of_lanes):
+                product = product + rows[:, q * LANES : (q + 1) * LANES] * vector[q]
+            return jnp.broadcast_to(jnp.sum(product, axis=1, keepdims=True), (8, LANES))
+
+        for side in range(2):
+            wait_for(in_vector.at[1 + side], recv_vector.at[1 + side], n_mem)
+        far_vectors = [vector_of(1), vector_of(2)]
+        wait_for(in_vector.at[0], recv_vector.at[0])
+        vector = vector_of(0)
         for c in range(3):
-            tile = jnp.where(lane == c, own[c], tile)
-        for m in range(n_mem):
-            out_small[CORRECTION, m] = tile
-        send(out_small, in_small, CORRECTION, send_small, recv_small)
-        in_small[CORRECTION, mem] = tile
-        for side in range(2):
-            for c in range(3):
-                out_plane[SWEEPS + 1, side, c] = jnp.concatenate([tile, tile], axis=0)
-            plane_copy(SWEEPS + 1, side).start()
-        for side in range(2):
-            plane_copy(SWEEPS + 1, side).wait_recv()
-        far = pick(plane_mat[...], in_plane[SWEEPS + 1, :, 0].reshape(32, LANES))
-        all_of(in_small, CORRECTION, recv_small)
-        near = pick(lift_mat[...], in_small[CORRECTION].reshape(wide, LANES))
-        for c in range(3):
-            mine = jnp.broadcast_to(own[c], (8, LANES))
-
-            def difference(values, start):
-                return mine - jnp.broadcast_to(values[start : start + 8, c : c + 1], (8, LANES))
-
-            gap = [difference(near, 8 * d) for d in range(4)]
-            gap_lower, gap_upper = difference(far, 0), difference(far, 16)
+            mine = correction(solver_rows[c], vector)
+            gap = [
+                mine - correction(near_rows[c, pl.ds(8 * d, 8), :], vector) for d in range(4)
+            ]
+            gap_lower, gap_upper = [
+                mine - correction(far_rows[c, side], far_vectors[side]) for side in range(2)
+            ]
             gap_k = jnp.where(first_k, gap[0], gap[1])
             for i in range(EDGE):
                 for v in range(2):
@@ -577,8 +637,23 @@
         packed = pick(pack_mat[...], side_by_side(lambda c: faces[c], 3))
         for c in range(3):
             out_big[t, :, c] = packed[:, c * LANES : (c + 1) * LANES].reshape(n_mem, 8, LANES)
-        send(out_big, in_big, t, send_big, recv_big)
+        send(out_big.at[t], in_big.at[t], send_big.at[t], recv_big.at[t])
         send_planes(t, 3, lambda c, i, v: step_dir[c, :, part(i, v)])
+
+        @pl.when(t < DEG)
+        def _():
+            for to in peers:
+                pltpu.make_async_remote_copy(
+                    src_ref=solver_rows.at[t],
+                    dst_ref=in_solver.at[t, mem],
+                    send_sem=send_solver.at[t],
+                    recv_sem=recv_solver.at[t],
+                    device_id={"mem": to},
+                    device_id_type=MESH,
+                ).start()
+            for side in range(2):
+                far_solver(t, side).start()
+
         in_big[t, mem] = out_big[t, mem]
 
         @pl.loop(0, 3)
@@ -608,8 +683,12 @@
                     )
                     velocity[c, :, part(i, v)] = velocity[c, :, part(i, v)] + x
 
+        @pl.when(t == SWEEPS - 1)
+        def _():
+            store(0).start()
+
         receive_planes(t, 3)
-        all_of(in_big, t, recv_big)
+        wait_for(in_big.at[t], recv_big.at[t])
         unpack_near(
             unpack_mat[...],
             side_by_side(lambda c: in_big[t, :, c].reshape(wide, LANES), 3),
@@ -624,15 +703,23 @@
             for v, value in enumerate(new(i)):
                 residual[c, :, part(i, v)] = value
 
-    span = in_face.at[pl.ds(0, n_mem - 1)]
-    pltpu.make_async_copy(span, span, send_face).wait()
+    store(1).start()
+    wait_for(in_face, send_face)
+    for t in range(SWEEPS):
+        wait_for(out_big.at[t], send_big.at[t])
+    for t in range(DEG):
+        wait_for(in_solver.at[t], send_solver.at[t])
+        for side in range(2):
+            far_solver(t, side).wait_send()
+    wait_for(in_vector.at[0], send_vector.at[0])
+    for side in range(2):
+        wait_for(in_vector.at[1 + side], send_vector.at[1 + side], n_mem)
+    wait_for(out_request, send_request)
     for t in range(SWEEPS + 1):
-        all_of(out_big, t, send_big)
-    for t in (REQUEST, CORRECTION):
-        all_of(out_small, t, send_small)
-    for t in range(SWEEPS + 2):
         for side in range(2):
             plane_copy(t, side).wait_send()
+    for place in range(2):
+        store(place).wait()
 
 
 def solution(mesh):
@@ -652,13 +739,16 @@
         field = pltpu.VMEM((8, CELLS), F32)
         vmem = pl.BlockSpec(memory_space=pltpu.VMEM)
         hbm = pl.BlockSpec(memory_space=pltpu.HBM)
+        smem = pl.BlockSpec(memory_space=pltpu.SMEM)
         dma = pltpu.SemaphoreType.DMA
         both = pl.pallas_call(
             functools.partial(kernel, n_grp, n_mem),
             out_shape=jax.ShapeDtypeStruct((2, *forcing.shape), F32),
-            in_specs=[hbm] * 3 + [vmem] * 5,
-            out_specs=vmem,
+            in_specs=[hbm] * 3 + [vmem] * 5 + [smem] * 2,
+            out_specs=hbm,
             scratch_shapes=[
+                pltpu.VMEM((3, 8, CELLS), F32),
+                pltpu.VMEM((3, 8, CELLS), F32),
                 field,
                 pltpu.VMEM((24, n_mem * 24), F32),
                 pltpu.VMEM((2, 8, CELLS), F32),
@@ -678,25 +768,38 @@
                 pltpu.VMEM((wide, 192), BF16),
                 pltpu.VMEM((32, 96), BF16),
                 pltpu.VMEM((32, 3 * wide), BF16),
-                pltpu.VMEM((64, 3 * n_mem * 64), BF16),
-                pltpu.VMEM((24, -(-n_mem * 24 // LANES) * LANES), F32),
+                pltpu.VMEM((2, 8, 8), F32),
+                pltpu.VMEM((3, 8, n_mem * 24), F32),
+                pltpu.VMEM((3, n_mem, 8, n_mem * 24), F32),
+                pltpu.VMEM((3, 2, 8, n_mem * 24), F32),
+                pltpu.VMEM((3, 32, n_mem * 24), F32),
+                pltpu.VMEM((3, 2, 8, n_mem * 24), F32),
+                pltpu.VMEM((8, LANES), F32),
+                pltpu.VMEM((3, n_mem, 8, LANES), F32),
                 pltpu.VMEM((64, LANES), F32),
                 pltpu.VMEM((n_mem, 64, LANES), F32),
-                pltpu.VMEM((SWEEPS + 1, n_mem, 3, 8, LANES), F32),
-                pltpu.VMEM((SWEEPS + 1, n_mem, 3, 8, LANES), F32),
-                pltpu.VMEM((2, n_mem, 8, LANES), F32),
-                pltpu.VMEM((2, n_mem, 8, LANES), F32),
-                pltpu.VMEM((SWEEPS + 2, 2, 3, 16, LANES), F32),
-                pltpu.VMEM((SWEEPS + 2, 2, 3, 16, LANES), F32),
-                dma((SWEEPS + 1,)),
-                dma((SWEEPS + 1,)),
-                dma((2,)),
-                dma((2,)),
-                dma((SWEEPS + 2, 2)),
-                dma((SWEEPS + 2, 2)),
+                pltpu.VMEM((SWEEPS, n_mem, 3, 8, LANES), F32),
+                pltpu.VMEM((SWEEPS, n_mem, 3, 8, LANES), F32),
+                pltpu.VMEM((n_mem, 8, LANES), F32),
+                pltpu.VMEM((n_mem, 8, LANES), F32),
+                pltpu.VMEM((SWEEPS + 1, 2, 3, 16, LANES), F32),
+                pltpu.VMEM((SWEEPS + 1, 2, 3, 16, LANES), F32),
+                dma((SWEEPS,)),
+                dma((SWEEPS,)),
                 dma,
                 dma,
+                dma((SWEEPS + 1, 2)),
+                dma((SWEEPS + 1, 2)),
+                dma,
+                dma,
+                dma((DEG,)),
+                dma((DEG,)),
+                dma((DEG, 2)),
+                dma((DEG, 2)),
                 dma((3,)),
+                dma((3,)),
+                dma((3,)),
+                dma((2,)),
             ],
             compiler_params=pltpu.CompilerParams(
                 collective_id=0, has_side_effects=True, vmem_limit_bytes=56 * 1024 * 1024
@@ -711,6 +814,8 @@
             face_block.T,
             plane_block.T,
             hanging,
+            face_owner.reshape(1, 32),
+            face_block.T,
         )
         return both[0], both[1]
 

time: 67.2 us -> 65.6 us (0.976)
  Pallas kernels: 64 us -> 62.7 us
    pallas_call x1, Pallas kernels: 64 us -> 62.7 us  [local(): pl.pallas_call(functools.partial(kernel, n_grp, n_mem), out_shape=jax.Sha...]
where the time goes in v3:
time: 65.6 us; the launch traced here: 65.4 us
  Pallas kernels  62.7 us (96%)
  local copies, waits for them, and re-layouts  2.04 us (3%)
    pallas_call x1, Pallas kernels, local(): pl.pallas_call(functools.partial(kernel, n_grp, n_mem), out_shape=jax.Sha...  62.7 us
    squeeze x1, local copies, waits for them, and re-layouts, local(): return (both[0], both[1])  2.04 us

profile of v3, /device:TPU:0, one launch (start us, length us, event | category | flops | bytes accessed | tf_op | source)
XLA Modules:
  0.0 65.4 jit_solution(7522246913147748969)
XLA Ops:
  0.6 62.7 %vcycle.1 = f32[2,3,8,4096]{3,2,1,0:T(8,128)} custom-call(f32[3,8,4096]{2,1,0:T(8,128)} %forcing_hbm.1, f32[8,4096]{1,0:T(8,128)} %viscosity_hbm.1, f32[1,24,384]{2,1,0:T(8,128)} %solver_hbm.1, s32[1,8]{1,0:T(1,128)} %bitcast.13, s32[1,32]{1,0:T(1,128)} %bitcast.10, s32[4,8]{1,0:T(4,128)} %bitcast.8, s32[2,8]{1,0:T(2,128)} %bitcast.12, s32[8,6]{1,0:T(8,128)} %hanging.1, ...), custom_call_target="tpu_custom_call" | custom-call | tf_op jit(solution)/shard_map/vcycle/pallas_call | solution.py:744
  63.4 2.0 %slice_bitcast_fusion = (f32[3,8,4096]{2,1,0:T(8,128)}, f32[3,8,4096]{2,1,0:T(8,128)}) fusion(f32[2,3,8,4096]{3,2,1,0:T(8,128)} %vcycle.1), kind=kLoop, calls=%fused_computation | loop fusion | bytes 1572864 | tf_op jit(solution)/shard_map/squeeze | solution.py:820

commit v4 on v3

--- a/solution.py
+++ b/solution.py
@@ -260,10 +260,7 @@
     for to in peers:
         pl.semaphore_signal(barrier, inc=1, device_id={"mem": to}, device_id_type=MESH)
     for other in (above, below):
-        for to in [*peers, mem]:
-            pl.semaphore_signal(
-                barrier, inc=1, device_id={"grp": other, "mem": to}, device_id_type=MESH
-            )
+        pl.semaphore_signal(barrier, inc=1, device_id={"grp": other}, device_id_type=MESH)
 
     loads = [
         pltpu.make_async_copy(viscosity_hbm, effective, load_sem.at[0]),
@@ -344,7 +341,7 @@
     for (v, d), register in found.items():
         out_face[pl.ds(v * 32 + d * 8, 8), :] = register
 
-    pl.semaphore_wait(barrier, n_mem - 1 + 2 * n_mem)
+    pl.semaphore_wait(barrier, n_mem - 1 + 2)
 
     for to in peers:
         pltpu.make_async_remote_copy(

time: 65.6 us -> 64.8 us (0.988)
  Pallas kernels: 62.7 us -> 61.7 us
    pallas_call x1, Pallas kernels: 62.7 us -> 61.7 us  [local(): pl.pallas_call(functools.partial(kernel, n_grp, n_mem), out_shape=jax.Sha...]
where the time goes in v4:
time: 64.8 us; the launch traced here: 64.4 us
  Pallas kernels  61.7 us (95%)
  local copies, waits for them, and re-layouts  2.04 us (3%)
    pallas_call x1, Pallas kernels, local(): pl.pallas_call(functools.partial(kernel, n_grp, n_mem), out_shape=jax.Sha...  61.7 us
    squeeze x1, local copies, waits for them, and re-layouts, local(): return (both[0], both[1])  2.04 us

profile of v4, /device:TPU:0, one launch (start us, length us, event | category | flops | bytes accessed | tf_op | source)
XLA Modules:
  0.0 64.4 jit_solution(17139698084426239320)
XLA Ops:
  0.6 61.7 %vcycle.1 = f32[2,3,8,4096]{3,2,1,0:T(8,128)} custom-call(f32[3,8,4096]{2,1,0:T(8,128)} %forcing_hbm.1, f32[8,4096]{1,0:T(8,128)} %viscosity_hbm.1, f32[1,24,384]{2,1,0:T(8,128)} %solver_hbm.1, s32[1,8]{1,0:T(1,128)} %bitcast.13, s32[1,32]{1,0:T(1,128)} %bitcast.10, s32[4,8]{1,0:T(4,128)} %bitcast.8, s32[2,8]{1,0:T(2,128)} %bitcast.12, s32[8,6]{1,0:T(8,128)} %hanging.1, ...), custom_call_target="tpu_custom_call" | custom-call | tf_op jit(solution)/shard_map/vcycle/pallas_call | solution.py:741
  62.4 2.0 %slice_bitcast_fusion = (f32[3,8,4096]{2,1,0:T(8,128)}, f32[3,8,4096]{2,1,0:T(8,128)}) fusion(f32[2,3,8,4096]{3,2,1,0:T(8,128)} %vcycle.1), kind=kLoop, calls=%fused_computation | loop fusion | bytes 1572864 | tf_op jit(solution)/shard_map/squeeze | solution.py:817

commit v5 on v4

--- a/solution.py
+++ b/solution.py
@@ -19,6 +19,7 @@
 LOWER_BOUND = 0.25
 UPPER_BOUND = 2.0
 SWEEPS = 2 * DEG
+GROUPS = ((0, 1, 2),)
 F32 = jnp.float32
 BF16 = jnp.bfloat16
 
@@ -183,6 +184,12 @@
     forcing_hbm,
     viscosity_hbm,
     solver_hbm,
+    refinement_hbm,
+    owner_hbm,
+    block_hbm,
+    plane_hbm,
+    hanging_hbm,
+    result,
     refinement,
     face_owner,
     face_block,
@@ -190,7 +197,6 @@
     hanging,
     owner_scalar,
     block_scalar,
-    result,
     velocity,
     residual,
     effective,
@@ -203,9 +209,8 @@
     diagonal,
     inverse,
     step_dir,
-    faces,
     ghosts,
-    plane_ghosts,
+    lifts,
     hang_near,
     hang_plane,
     unpack_mat,
@@ -222,14 +227,10 @@
     in_vector,
     out_face,
     in_face,
-    out_big,
-    in_big,
     out_request,
     in_request,
     out_plane,
     in_plane,
-    send_big,
-    recv_big,
     send_request,
     recv_request,
     send_plane,
@@ -244,11 +245,13 @@
     recv_vector,
     load_sem,
     store_sem,
+    *group_refs,
 ):
     grp, mem = lax.axis_index("grp"), lax.axis_index("mem")
     above = lax.rem(grp + 1, n_grp)
     below = lax.rem(grp + n_grp - 1, n_grp)
     n_coarse = n_mem * 24
+    buffers = [group_refs[8 * g : 8 * g + 8] for g in range(len(GROUPS))]
     groups_of_lanes = n_coarse // LANES
     wide = n_mem * 8
 
@@ -267,7 +270,20 @@
         pltpu.make_async_copy(forcing_hbm, residual, load_sem.at[1]),
         pltpu.make_async_copy(solver_hbm.at[0], solver, load_sem.at[2]),
     ]
-    for load in loads:
+    small = [
+        (refinement_hbm, refinement),
+        (owner_hbm, face_owner),
+        (block_hbm, face_block),
+        (plane_hbm, plane_block),
+        (hanging_hbm, hanging),
+        (owner_hbm, owner_scalar),
+        (block_hbm, block_scalar),
+    ]
+    small = [
+        pltpu.make_async_copy(source, target, load_sem.at[3 + place])
+        for place, (source, target) in enumerate(small)
+    ]
+    for load in [*small, *loads]:
         load.start()
 
     def store(place):
@@ -295,15 +311,21 @@
         span = buffer.at[pl.ds(0, count)]
         pltpu.make_async_copy(span, span, sem).wait()
 
-    def plane_copy(which, side):
+    def plane_copy(side, outgoing, incoming, send_sem, recv_sem):
         return pltpu.make_async_remote_copy(
-            src_ref=out_plane.at[which, side],
-            dst_ref=in_plane.at[which, side],
-            send_sem=send_plane.at[which, side],
-            recv_sem=recv_plane.at[which, side],
+            src_ref=outgoing.at[side],
+            dst_ref=incoming.at[side],
+            send_sem=send_sem.at[side],
+            recv_sem=recv_sem.at[side],
             device_id={"grp": above if side == 0 else below},
             device_id_type=MESH,
         )
+
+    def effective_plane(side):
+        return plane_copy(side, out_plane, in_plane, send_plane, recv_plane)
+
+    def step_plane(g, t, side):
+        return plane_copy(side, *[ref.at[t] for ref in buffers[g][4:]])
 
     def far_solver(c, side):
         return pltpu.make_async_remote_copy(
@@ -314,6 +336,9 @@
             device_id={"grp": above if side == 0 else below},
             device_id_type=MESH,
         )
+
+    for load in small:
+        load.wait()
 
     block_row = iota((8, LANES), 0)
     level = jnp.sum(
@@ -326,34 +351,10 @@
         for v in range(2):
             effective[:, part(i, v)] = effective[:, part(i, v)] * scale
 
-    def send_planes(which, channels, read):
-        for c in range(channels):
-            for v in range(2):
-                out_plane[which, 0, c, pl.ds(8 * v, 8), :] = read(c, EDGE - 1, v)
-                out_plane[which, 1, c, pl.ds(8 * v, 8), :] = read(c, 0, v)
-        for side in range(2):
-            plane_copy(which, side).start()
-
-    for side in range(2):
-        for c in range(1, 3):
-            out_plane[SWEEPS, side, c] = jnp.zeros((16, LANES), F32)
     found = extract(lambda i, v: effective[:, part(i, v)])
     for (v, d), register in found.items():
         out_face[pl.ds(v * 32 + d * 8, 8), :] = register
 
-    pl.semaphore_wait(barrier, n_mem - 1 + 2)
-
-    for to in peers:
-        pltpu.make_async_remote_copy(
-            src_ref=out_face,
-            dst_ref=in_face.at[mem],
-            send_sem=send_face,
-            recv_sem=recv_face,
-            device_id={"mem": to},
-            device_id_type=MESH,
-        ).start()
-    send_planes(SWEEPS, 1, lambda c, i, v: effective[:, part(i, v)])
-    in_face[mem] = out_face[...]
     unpack, request, plane_pick, lift_pick, far_pick, near_hang, plane_hang = tables(
         face_owner[...],
         face_block[...],
@@ -371,7 +372,25 @@
     hang_near[...] = near_hang
     hang_plane[...] = plane_hang
     out_request[...] = request.reshape(n_mem, 8, LANES)
+
+    pl.semaphore_wait(barrier, n_mem - 1 + 2)
+
     send(out_request, in_request, send_request, recv_request)
+    for to in peers:
+        pltpu.make_async_remote_copy(
+            src_ref=out_face,
+            dst_ref=in_face.at[mem],
+            send_sem=send_face,
+            recv_sem=recv_face,
+            device_id={"mem": to},
+            device_id_type=MESH,
+        ).start()
+    for v in range(2):
+        out_plane[0, pl.ds(8 * v, 8), :] = effective[:, part(EDGE - 1, v)]
+        out_plane[1, pl.ds(8 * v, 8), :] = effective[:, part(0, v)]
+    for side in range(2):
+        effective_plane(side).start()
+    in_face[mem] = out_face[...]
     in_request[mem] = out_request[mem]
 
     loads[1].wait()
@@ -385,7 +404,6 @@
         for i in range(EDGE):
             for v in range(2):
                 velocity[c, :, part(i, v)] = jnp.zeros((8, LANES), F32)
-                step_dir[c, :, part(i, v)] = jnp.zeros((8, LANES), F32)
     for i in range(EDGE):
         own = [effective[:, part(i, v)] for v in range(2)]
         back = [turn(x, EDGE) for x in own]
@@ -411,38 +429,47 @@
     def settle(values, hang):
         return jnp.where(hang == 1.0, coarsen(values), values)
 
-    def side_by_side(buffer, channels):
-        return jnp.concatenate([buffer(c) for c in range(channels)], axis=1)
-
-    def receive_planes(which, channels):
+    def side_by_side(pieces):
+        return pieces[0] if len(pieces) == 1 else jnp.concatenate(pieces, axis=1)
+
+    def columns(values, count):
+        return [values[:, l * LANES : (l + 1) * LANES] for l in range(count)]
+
+    def receive(g, t):
+        count = len(GROUPS[g])
+        incoming, recv_sem, planes = buffers[g][1], buffers[g][3], buffers[g][5]
         for side in range(2):
-            plane_copy(which, side).wait_recv()
-        arrived = side_by_side(
-            lambda c: in_plane[which, :, c].reshape(32, LANES), channels
+            step_plane(g, t, side).wait_recv()
+        far = pick(
+            plane_mat[...],
+            side_by_side([planes[t, :, l].reshape(32, LANES) for l in range(count)]),
         )
-        picked = pick(plane_mat[...], arrived)
-        for c in range(channels):
-            plane_ghosts[c] = settle(picked[:, c * LANES : (c + 1) * LANES], hang_plane[...])
-
-    def unpack_near(matrix, arrived, channels):
-        picked = pick(matrix, arrived)
-        for c in range(channels):
-            for v in range(2):
-                ghosts[c, pl.ds(32 * v, 32), :] = settle(
-                    picked[32 * v : 32 * v + 32, c * LANES : (c + 1) * LANES], hang_near[...]
+        far = [settle(values, hang_plane[...]) for values in columns(far, count)]
+        wait_for(incoming.at[t], recv_sem.at[t])
+        near = pick(
+            unpack_mat[...],
+            side_by_side([incoming[t, :, l].reshape(wide, LANES) for l in range(count)]),
+        )
+        result = []
+        for l, values in enumerate(columns(near, count)):
+            halves = [settle(values[32 * v : 32 * v + 32], hang_near[...]) for v in range(2)]
+            result.append(
+                (
+                    {(d, v): halves[v][8 * d : 8 * d + 8] for d in range(4) for v in range(2)},
+                    {
+                        (side, v): far[l][16 * side + 8 * v : 16 * side + 8 * v + 8]
+                        for side in range(2)
+                        for v in range(2)
+                    },
                 )
-
-    def ghost(c, d, v):
-        return ghosts[c, pl.ds(v * 32 + d * 8, 8), :]
-
-    def plane_ghost(c, side, v):
-        return plane_ghosts[c, pl.ds(side * 16 + v * 8, 8), :]
-
-    def near_ghosts(c):
-        lower_k = [ghost(c, 0, v) for v in range(2)]
-        upper_k = [turn(ghost(c, 1, v), EDGE - 1) for v in range(2)]
-        lower_j = [ghost(c, 2, v) for v in range(2)]
-        upper_j = [turn(ghost(c, 3, v), LANES - EDGE) for v in range(2)]
+            )
+        return result
+
+    def near_ghosts(near):
+        lower_k = [near[0, v] for v in range(2)]
+        upper_k = [turn(near[1, v], EDGE - 1) for v in range(2)]
+        lower_j = [near[2, v] for v in range(2)]
+        upper_j = [turn(near[3, v], LANES - EDGE) for v in range(2)]
 
         def at_k(i, v):
             return turn(jnp.where(in_row == i, lower_k[v], upper_k[v]), -i)
@@ -453,22 +480,27 @@
 
         return at_k, at_j
 
-    receive_planes(SWEEPS, 1)
+    for side in range(2):
+        effective_plane(side).wait_recv()
+    far = settle(pick(plane_mat[...], in_plane[...].reshape(32, LANES)), hang_plane[...])
     for v in range(2):
-        weight_i[:, part(0, v)] = 0.5 * (effective[:, part(0, v)] + plane_ghost(0, 0, v))
-        weight_i[:, part(EDGE, v)] = 0.5 * (effective[:, part(EDGE - 1, v)] + plane_ghost(0, 1, v))
+        weight_i[:, part(0, v)] = 0.5 * (effective[:, part(0, v)] + far[8 * v : 8 * v + 8])
+        weight_i[:, part(EDGE, v)] = 0.5 * (
+            effective[:, part(EDGE - 1, v)] + far[16 + 8 * v : 24 + 8 * v]
+        )
     wait_for(in_face, recv_face)
     for d in range(4):
         for b in range(8):
             owner = owner_scalar[0, 4 * b + d]
             wanted = (d + 1 - 2 * (d % 2)) * 8 + block_scalar[d, b]
             for v in range(2):
-                ghosts[0, pl.ds(v * 32 + d * 8 + b, 1), :] = in_face[
+                ghosts[pl.ds(v * 32 + d * 8 + b, 1), :] = in_face[
                     owner, pl.ds(v * 32 + wanted, 1), :
                 ]
-    for v in range(2):
-        ghosts[0, pl.ds(32 * v, 32), :] = settle(ghosts[0, pl.ds(32 * v, 32), :], hang_near[...])
-    k_ghost, j_ghost = near_ghosts(0)
+    halves = [settle(ghosts[pl.ds(32 * v, 32), :], hang_near[...]) for v in range(2)]
+    k_ghost, j_ghost = near_ghosts(
+        {(d, v): halves[v][8 * d : 8 * d + 8] for d in range(4) for v in range(2)}
+    )
     for i in range(EDGE):
         beside_j = j_ghost(i)
         for v in range(2):
@@ -487,14 +519,12 @@
             inverse[:, part(i, v)] = 1.0 / whole
 
     steps = chebyshev()
-    ghosts[...] = jnp.zeros(ghosts.shape, F32)
-    plane_ghosts[...] = jnp.zeros(plane_ghosts.shape, F32)
     wait_for(in_request, recv_request)
     request = in_request[...].reshape(wide, LANES)
     pack_mat[...] = jnp.concatenate([request, request[:, :64]], axis=1).astype(BF16)
 
-    def across_faces(c):
-        k_ghost, j_ghost = near_ghosts(c)
+    def across_faces(c, near, far):
+        k_ghost, j_ghost = near_ghosts(near)
 
         def new(i):
             beside_j = j_ghost(i)
@@ -503,24 +533,25 @@
                 change = ghost_k[:, part(i, v)] * k_ghost(i, v)
                 change = change + ghost_j[:, part(i, v)] * beside_j
                 if i == 0:
-                    change = change + weight_i[:, part(0, v)] * plane_ghost(c, 0, v)
+                    change = change + weight_i[:, part(0, v)] * far[0, v]
                 if i == EDGE - 1:
-                    change = change + weight_i[:, part(EDGE, v)] * plane_ghost(c, 1, v)
+                    change = change + weight_i[:, part(EDGE, v)] * far[1, v]
                 result.append(residual[c, :, part(i, v)] + change)
             return result
 
         return new
 
     def coarse_level():
-        totals = []
-        for c in range(3):
-            total = jnp.zeros((8, LANES), F32)
-            new = across_faces(c)
-            for i in range(EDGE):
-                for v, value in enumerate(new(i)):
-                    residual[c, :, part(i, v)] = value
-                    total = total + value
-            totals.append(jnp.sum(total, axis=1, keepdims=True) / math.sqrt(CELLS))
+        totals = [None] * 3
+        for g, group in enumerate(GROUPS):
+            for c, arrived in zip(group, receive(g, DEG - 1)):
+                total = jnp.zeros((8, LANES), F32)
+                new = across_faces(c, *arrived)
+                for i in range(EDGE):
+                    for v, value in enumerate(new(i)):
+                        residual[c, :, part(i, v)] = value
+                        total = total + value
+                totals[c] = jnp.sum(total, axis=1, keepdims=True) / math.sqrt(CELLS)
         chunks = []
         for q in range(groups_of_lanes):
             place = lane + q * LANES - 24 * mem - 3 * block_row
@@ -581,16 +612,17 @@
         far_vectors = [vector_of(1), vector_of(2)]
         wait_for(in_vector.at[0], recv_vector.at[0])
         vector = vector_of(0)
-        for c in range(3):
+        def lifted(c):
             mine = correction(solver_rows[c], vector)
-            gap = [
-                mine - correction(near_rows[c, pl.ds(8 * d, 8), :], vector) for d in range(4)
-            ]
+            lifts[c] = mine
+            gap = [mine - correction(near_rows[c, pl.ds(8 * d, 8), :], vector) for d in range(4)]
             gap_lower, gap_upper = [
                 mine - correction(far_rows[c, side], far_vectors[side]) for side in range(2)
             ]
             gap_k = jnp.where(first_k, gap[0], gap[1])
-            for i in range(EDGE):
+
+            def new(i):
+                result = []
                 for v in range(2):
                     change = MASS_TERM * effective[:, part(i, v)] * mine
                     change = change + ghost_k[:, part(i, v)] * gap_k
@@ -599,60 +631,62 @@
                         change = change + weight_i[:, part(0, v)] * gap_lower
                     if i == EDGE - 1:
                         change = change + weight_i[:, part(EDGE, v)] * gap_upper
-                    residual[c, :, part(i, v)] = residual[c, :, part(i, v)] - change
-                    velocity[c, :, part(i, v)] = velocity[c, :, part(i, v)] + mine
-        ghosts[...] = jnp.zeros(ghosts.shape, F32)
-        plane_ghosts[...] = jnp.zeros(plane_ghosts.shape, F32)
-
-    def sweep(t, carry):
-        @pl.when(t == DEG)
-        def _():
-            coarse_level()
-
-        step = lax.rem(t, DEG)
-        keep = by_step(step, [first for first, _ in steps])
-        gain = by_step(step, [second for _, second in steps])
-
-        for c in range(3):
-            new = across_faces(c)
+                    result.append(residual[c, :, part(i, v)] - change)
+                return result
+
+            return new
+
+        return lifted
+
+    def advance(g, t, news, keep, gain):
+        outgoing, incoming, send_sem, recv_sem, planes = buffers[g][:5]
+        group = GROUPS[g]
+        columns_out = []
+        for l, c in enumerate(group):
             moved = {}
 
             def step_of(i, v):
                 if v == 0:
-                    for half, value in enumerate(new(i)):
-                        residual[c, :, part(i, half)] = value
-                        ahead = keep * step_dir[c, :, part(i, half)] + gain * (
-                            value * inverse[:, part(i, half)]
-                        )
+                    for half, value in enumerate(news[l](i)):
+                        if keep is not None or t == DEG:
+                            residual[c, :, part(i, half)] = value
+                        ahead = gain * (value * inverse[:, part(i, half)])
+                        if keep is not None:
+                            ahead = keep * step_dir[c, :, part(i, half)] + ahead
                         step_dir[c, :, part(i, half)] = ahead
                         moved[i, half] = ahead
                 return moved[i, v]
 
-            for (v, d), register in extract(step_of).items():
-                faces[c, pl.ds(v * 32 + d * 8, 8), :] = register
-
-        packed = pick(pack_mat[...], side_by_side(lambda c: faces[c], 3))
-        for c in range(3):
-            out_big[t, :, c] = packed[:, c * LANES : (c + 1) * LANES].reshape(n_mem, 8, LANES)
-        send(out_big.at[t], in_big.at[t], send_big.at[t], recv_big.at[t])
-        send_planes(t, 3, lambda c, i, v: step_dir[c, :, part(i, v)])
-
-        @pl.when(t < DEG)
-        def _():
-            for to in peers:
-                pltpu.make_async_remote_copy(
-                    src_ref=solver_rows.at[t],
-                    dst_ref=in_solver.at[t, mem],
-                    send_sem=send_solver.at[t],
-                    recv_sem=recv_solver.at[t],
-                    device_id={"mem": to},
-                    device_id_type=MESH,
-                ).start()
-            for side in range(2):
-                far_solver(t, side).start()
-
-        in_big[t, mem] = out_big[t, mem]
-
+            found = extract(step_of)
+            columns_out.append(
+                jnp.concatenate([found[v, d] for v in range(2) for d in range(4)], axis=0)
+            )
+        packed = columns(pick(pack_mat[...], side_by_side(columns_out)), len(group))
+        for l in range(len(group)):
+            outgoing[t, :, l] = packed[l].reshape(n_mem, 8, LANES)
+        send(outgoing.at[t], incoming.at[t], send_sem.at[t], recv_sem.at[t])
+        for l, c in enumerate(group):
+            for v in range(2):
+                planes[t, 0, l, pl.ds(8 * v, 8), :] = step_dir[c, :, part(EDGE - 1, v)]
+                planes[t, 1, l, pl.ds(8 * v, 8), :] = step_dir[c, :, part(0, v)]
+        for side in range(2):
+            step_plane(g, t, side).start()
+        incoming[t, mem] = outgoing[t, mem]
+
+    def send_solver_rows(c):
+        for to in peers:
+            pltpu.make_async_remote_copy(
+                src_ref=solver_rows.at[c],
+                dst_ref=in_solver.at[c, mem],
+                send_sem=send_solver.at[c],
+                recv_sem=recv_solver.at[c],
+                device_id={"mem": to},
+                device_id_type=MESH,
+            ).start()
+        for side in range(2):
+            far_solver(c, side).start()
+
+    def inside(lift):
         @pl.loop(0, 3)
         def _(c):
             for i in range(EDGE):
@@ -678,32 +712,54 @@
                     residual[c, :, part(i, v)] = residual[c, :, part(i, v)] - (
                         diagonal[:, part(i, v)] * x - change
                     )
+                    if lift:
+                        x = x + lifts[c]
                     velocity[c, :, part(i, v)] = velocity[c, :, part(i, v)] + x
 
-        @pl.when(t == SWEEPS - 1)
-        def _():
-            store(0).start()
-
-        receive_planes(t, 3)
-        wait_for(in_big.at[t], recv_big.at[t])
-        unpack_near(
-            unpack_mat[...],
-            side_by_side(lambda c: in_big[t, :, c].reshape(wide, LANES), 3),
-            3,
-        )
-        return carry
-
-    lax.fori_loop(0, SWEEPS, sweep, 0)
-    for c in range(3):
-        new = across_faces(c)
-        for i in range(EDGE):
-            for v, value in enumerate(new(i)):
-                residual[c, :, part(i, v)] = value
+    def as_is(c):
+        return lambda i: [residual[c, :, part(i, v)] for v in range(2)]
+
+    def later(first):
+        def sweep(t, carry):
+            keep = by_step(t - first, [value for value, _ in steps])
+            gain = by_step(t - first, [value for _, value in steps])
+            for g, group in enumerate(GROUPS):
+                news = [
+                    across_faces(c, *arrived) for c, arrived in zip(group, receive(g, t - 1))
+                ]
+                advance(g, t, news, keep, gain)
+            if first == 0:
+                send_solver_rows(t)
+            inside(False)
+            return carry
+
+        lax.fori_loop(first + 1, first + DEG, sweep, 0)
+
+    for g, group in enumerate(GROUPS):
+        advance(g, 0, [as_is(c) for c in group], None, jnp.float32(steps[0][1]))
+    send_solver_rows(0)
+    inside(False)
+    later(0)
+    lifted = coarse_level()
+    for g, group in enumerate(GROUPS):
+        advance(g, DEG, [lifted(c) for c in group], None, jnp.float32(steps[0][1]))
+    inside(True)
+    later(DEG)
+    store(0).start()
+    for g, group in enumerate(GROUPS):
+        for c, arrived in zip(group, receive(g, SWEEPS - 1)):
+            new = across_faces(c, *arrived)
+            for i in range(EDGE):
+                for v, value in enumerate(new(i)):
+                    residual[c, :, part(i, v)] = value
 
     store(1).start()
     wait_for(in_face, send_face)
-    for t in range(SWEEPS):
-        wait_for(out_big.at[t], send_big.at[t])
+    for g in range(len(GROUPS)):
+        for t in range(SWEEPS):
+            wait_for(buffers[g][0].at[t], buffers[g][2].at[t])
+            for side in range(2):
+                step_plane(g, t, side).wait_send()
     for t in range(DEG):
         wait_for(in_solver.at[t], send_solver.at[t])
         for side in range(2):
@@ -712,11 +768,21 @@
     for side in range(2):
         wait_for(in_vector.at[1 + side], send_vector.at[1 + side], n_mem)
     wait_for(out_request, send_request)
-    for t in range(SWEEPS + 1):
-        for side in range(2):
-            plane_copy(t, side).wait_send()
+    for side in range(2):
+        effective_plane(side).wait_send()
     for place in range(2):
         store(place).wait()
+
+
+def group_scratch(n_mem):
+    shapes = []
+    for group in GROUPS:
+        near = pltpu.VMEM((SWEEPS, n_mem, len(group), 8, LANES), F32)
+        far = pltpu.VMEM((SWEEPS, 2, len(group), 16, LANES), F32)
+        dma = pltpu.SemaphoreType.DMA
+        shapes += [near, near, dma((SWEEPS,)), dma((SWEEPS,))]
+        shapes += [far, far, dma((SWEEPS, 2)), dma((SWEEPS, 2))]
+    return shapes
 
 
 def solution(mesh):
@@ -734,16 +800,21 @@
         coarse_solver,
     ):
         field = pltpu.VMEM((8, CELLS), F32)
-        vmem = pl.BlockSpec(memory_space=pltpu.VMEM)
         hbm = pl.BlockSpec(memory_space=pltpu.HBM)
-        smem = pl.BlockSpec(memory_space=pltpu.SMEM)
         dma = pltpu.SemaphoreType.DMA
         both = pl.pallas_call(
             functools.partial(kernel, n_grp, n_mem),
             out_shape=jax.ShapeDtypeStruct((2, *forcing.shape), F32),
-            in_specs=[hbm] * 3 + [vmem] * 5 + [smem] * 2,
+            in_specs=[hbm] * 8,
             out_specs=hbm,
             scratch_shapes=[
+                pltpu.VMEM((1, 8), jnp.int32),
+                pltpu.VMEM((1, 32), jnp.int32),
+                pltpu.VMEM((4, 8), jnp.int32),
+                pltpu.VMEM((2, 8), jnp.int32),
+                pltpu.VMEM((8, 6), jnp.int32),
+                pltpu.SMEM((1, 32), jnp.int32),
+                pltpu.SMEM((4, 8), jnp.int32),
                 pltpu.VMEM((3, 8, CELLS), F32),
                 pltpu.VMEM((3, 8, CELLS), F32),
                 field,
@@ -756,9 +827,8 @@
                 field,
                 field,
                 pltpu.VMEM((3, 8, CELLS), F32),
-                pltpu.VMEM((3, 64, LANES), F32),
-                pltpu.VMEM((3, 64, LANES), F32),
-                pltpu.VMEM((3, 32, LANES), F32),
+                pltpu.VMEM((64, LANES), F32),
+                pltpu.VMEM((3, 8, LANES), F32),
                 pltpu.VMEM((32, LANES), F32),
                 pltpu.VMEM((32, LANES), F32),
                 pltpu.VMEM((64, 3 * wide), BF16),
@@ -775,18 +845,14 @@
                 pltpu.VMEM((3, n_mem, 8, LANES), F32),
                 pltpu.VMEM((64, LANES), F32),
                 pltpu.VMEM((n_mem, 64, LANES), F32),
-                pltpu.VMEM((SWEEPS, n_mem, 3, 8, LANES), F32),
-                pltpu.VMEM((SWEEPS, n_mem, 3, 8, LANES), F32),
                 pltpu.VMEM((n_mem, 8, LANES), F32),
                 pltpu.VMEM((n_mem, 8, LANES), F32),
-                pltpu.VMEM((SWEEPS + 1, 2, 3, 16, LANES), F32),
-                pltpu.VMEM((SWEEPS + 1, 2, 3, 16, LANES), F32),
-                dma((SWEEPS,)),
-                dma((SWEEPS,)),
+                pltpu.VMEM((2, 16, LANES), F32),
+                pltpu.VMEM((2, 16, LANES), F32),
                 dma,
                 dma,
-                dma((SWEEPS + 1, 2)),
-                dma((SWEEPS + 1, 2)),
+                dma((2,)),
+                dma((2,)),
                 dma,
                 dma,
                 dma((DEG,)),
@@ -795,8 +861,9 @@
                 dma((DEG, 2)),
                 dma((3,)),
                 dma((3,)),
-                dma((3,)),
+                dma((10,)),
                 dma((2,)),
+                *group_scratch(n_mem),
             ],
             compiler_params=pltpu.CompilerParams(
                 collective_id=0, has_side_effects=True, vmem_limit_bytes=56 * 1024 * 1024
@@ -811,8 +878,6 @@
             face_block.T,
             plane_block.T,
             hanging,
-            face_owner.reshape(1, 32),
-            face_block.T,
         )
         return both[0], both[1]
 

time: 64.8 us -> 62.9 us (0.971)
  Pallas kernels: 61.7 us -> 59.7 us
    pallas_call x1, Pallas kernels: 61.7 us -> 59.7 us  [local(): pl.pallas_call(functools.partial(kernel, n_grp, n_mem), out_shape=jax.Sha...]
where the time goes in v5:
time: 62.9 us; the launch traced here: 62.4 us
  Pallas kernels  59.7 us (95%)
  local copies, waits for them, and re-layouts  2.04 us (3%)
  between operations  0.64 us (1%)
    pallas_call x1, Pallas kernels, local(): pl.pallas_call(functools.partial(kernel, n_grp, n_mem), out_shape=jax.Sha...  59.7 us
    squeeze x1, local copies, waits for them, and re-layouts, local(): return (both[0], both[1])  2.04 us

profile of v5, /device:TPU:0, one launch (start us, length us, event | category | flops | bytes accessed | tf_op | source)
XLA Modules:
  0.0 62.4 jit_solution(4979988555267653189)
XLA Ops:
  0.6 59.7 %vcycle.1 = f32[2,3,8,4096]{3,2,1,0:T(8,128)} custom-call(f32[3,8,4096]{2,1,0:T(8,128)} %forcing_hbm.1, f32[8,4096]{1,0:T(8,128)} %viscosity_hbm.1, f32[1,24,384]{2,1,0:T(8,128)} %solver_hbm.1, s32[1,8]{1,0:T(1,128)} %bitcast.10, s32[1,32]{1,0:T(1,128)} %bitcast.11, s32[4,8]{1,0:T(4,128)} %bitcast.8, s32[2,8]{1,0:T(2,128)} %bitcast.9, s32[8,6]{1,0:T(8,128)} %hanging_hbm.1), custom_call_target="tpu_custom_call" | custom-call | tf_op jit(solution)/shard_map/vcycle/pallas_call | solution.py:805
  60.4 2.0 %slice_bitcast_fusion = (f32[3,8,4096]{2,1,0:T(8,128)}, f32[3,8,4096]{2,1,0:T(8,128)}) fusion(f32[2,3,8,4096]{3,2,1,0:T(8,128)} %vcycle.1), kind=kLoop, calls=%fused_computation | loop fusion | bytes 1572864 | tf_op jit(solution)/shard_map/squeeze | solution.py:882

commit v6 on v5

--- a/solution.py
+++ b/solution.py
@@ -19,7 +19,7 @@
 LOWER_BOUND = 0.25
 UPPER_BOUND = 2.0
 SWEEPS = 2 * DEG
-GROUPS = ((0, 1, 2),)
+GROUPS = ((0,), (1, 2))
 F32 = jnp.float32
 BF16 = jnp.bfloat16
 
@@ -84,8 +84,8 @@
     return jnp.dot(one_hot_thrice, parts(values), preferred_element_type=F32)
 
 
-def coarsen(x):
-    lane = iota(x.shape, 1)
+def coarsen(x, start):
+    lane = (iota(x.shape, 1) + (LANES - start)) % LANES
     x = x + jnp.where(lane % 2 == 0, turn(x, -1), turn(x, 1))
     x = x + jnp.where(lane // EDGE % 2 == 0, turn(x, -EDGE), turn(x, EDGE))
     return 0.25 * x
@@ -107,7 +107,6 @@
         faces[v, 2] = jnp.where(row == i % 8, moved, faces[v, 2])
         faces[v, 3] = jnp.where(row == (i - 1) % 8, moved, faces[v, 3])
     for v in range(2):
-        faces[v, 1] = turn(faces[v, 1], -(EDGE - 1))
         faces[v, 3] = turn(faces[v, 3], EDGE)
     return faces
 
@@ -286,9 +285,11 @@
     for load in [*small, *loads]:
         load.start()
 
-    def store(place):
+    def store(place, c):
         source = (velocity, residual)[place]
-        return pltpu.make_async_copy(source, result.at[place], store_sem.at[place])
+        return pltpu.make_async_copy(
+            source.at[c], result.at[place, c], store_sem.at[place, c]
+        )
 
     lane = iota((8, LANES), 1)
     in_row = lane % EDGE
@@ -426,8 +427,10 @@
                 weight_i[:, part(i, v)] = 0.5 * (x + effective[:, part(i - 1, v)])
             diagonal[:, part(i, v)] = MASS_TERM * x + lower_k + upper_k + lower_j + upper_j
 
-    def settle(values, hang):
-        return jnp.where(hang == 1.0, coarsen(values), values)
+    def settle(values, hang, start=0):
+        return jnp.where(hang == 1.0, coarsen(values, start), values)
+
+    first_side = jnp.where(iota((32, LANES), 0) < 8, EDGE - 1, 0)
 
     def side_by_side(pieces):
         return pieces[0] if len(pieces) == 1 else jnp.concatenate(pieces, axis=1)
@@ -452,7 +455,7 @@
         )
         result = []
         for l, values in enumerate(columns(near, count)):
-            halves = [settle(values[32 * v : 32 * v + 32], hang_near[...]) for v in range(2)]
+            halves = [settle(values[32 * v : 32 * v + 32], hang_near[...], first_side) for v in range(2)]
             result.append(
                 (
                     {(d, v): halves[v][8 * d : 8 * d + 8] for d in range(4) for v in range(2)},
@@ -466,13 +469,13 @@
         return result
 
     def near_ghosts(near):
-        lower_k = [near[0, v] for v in range(2)]
-        upper_k = [turn(near[1, v], EDGE - 1) for v in range(2)]
+        lower_k = [turn(near[0, v], -2 * (EDGE - 1)) for v in range(2)]
+        upper_k = [near[1, v] for v in range(2)]
         lower_j = [near[2, v] for v in range(2)]
         upper_j = [turn(near[3, v], LANES - EDGE) for v in range(2)]
 
         def at_k(i, v):
-            return turn(jnp.where(in_row == i, lower_k[v], upper_k[v]), -i)
+            return turn(jnp.where(in_row == i, upper_k[v], lower_k[v]), EDGE - 1 - i)
 
         def at_j(i):
             both = jnp.where(row == i % 8, lower_j[i // 8], upper_j[i // 8])
@@ -497,7 +500,7 @@
                 ghosts[pl.ds(v * 32 + d * 8 + b, 1), :] = in_face[
                     owner, pl.ds(v * 32 + wanted, 1), :
                 ]
-    halves = [settle(ghosts[pl.ds(32 * v, 32), :], hang_near[...]) for v in range(2)]
+    halves = [settle(ghosts[pl.ds(32 * v, 32), :], hang_near[...], first_side) for v in range(2)]
     k_ghost, j_ghost = near_ghosts(
         {(d, v): halves[v][8 * d : 8 * d + 8] for d in range(4) for v in range(2)}
     )
@@ -728,32 +731,33 @@
                     across_faces(c, *arrived) for c, arrived in zip(group, receive(g, t - 1))
                 ]
                 advance(g, t, news, keep, gain)
+            inside(False)
             if first == 0:
                 send_solver_rows(t)
-            inside(False)
             return carry
 
         lax.fori_loop(first + 1, first + DEG, sweep, 0)
 
     for g, group in enumerate(GROUPS):
         advance(g, 0, [as_is(c) for c in group], None, jnp.float32(steps[0][1]))
+    inside(False)
     send_solver_rows(0)
-    inside(False)
     later(0)
     lifted = coarse_level()
     for g, group in enumerate(GROUPS):
         advance(g, DEG, [lifted(c) for c in group], None, jnp.float32(steps[0][1]))
     inside(True)
     later(DEG)
-    store(0).start()
+    for c in range(3):
+        store(0, c).start()
     for g, group in enumerate(GROUPS):
         for c, arrived in zip(group, receive(g, SWEEPS - 1)):
             new = across_faces(c, *arrived)
             for i in range(EDGE):
                 for v, value in enumerate(new(i)):
                     residual[c, :, part(i, v)] = value
-
-    store(1).start()
+            store(1, c).start()
+
     wait_for(in_face, send_face)
     for g in range(len(GROUPS)):
         for t in range(SWEEPS):
@@ -771,7 +775,8 @@
     for side in range(2):
         effective_plane(side).wait_send()
     for place in range(2):
-        store(place).wait()
+        for c in range(3):
+            store(place, c).wait()
 
 
 def group_scratch(n_mem):
@@ -862,7 +867,7 @@
                 dma((3,)),
                 dma((3,)),
                 dma((10,)),
-                dma((2,)),
+                dma((2, 3)),
                 *group_scratch(n_mem),
             ],
             compiler_params=pltpu.CompilerParams(

time: 62.9 us -> 61.9 us (0.984)
  Pallas kernels: 59.7 us -> 58.9 us
    pallas_call x1, Pallas kernels: 59.7 us -> 58.9 us  [local(): pl.pallas_call(functools.partial(kernel, n_grp, n_mem), out_shape=jax.Sha...]
where the time goes in v6:
time: 61.9 us; the launch traced here: 61.5 us
  Pallas kernels  58.9 us (95%)
  local copies, waits for them, and re-layouts  2.04 us (3%)
  between operations  0.64 us (1%)
    pallas_call x1, Pallas kernels, local(): pl.pallas_call(functools.partial(kernel, n_grp, n_mem), out_shape=jax.Sha...  58.9 us
    squeeze x1, local copies, waits for them, and re-layouts, local(): return (both[0], both[1])  2.04 us

profile of v6, /device:TPU:0, one launch (start us, length us, event | category | flops | bytes accessed | tf_op | source)
XLA Modules:
  0.0 61.5 jit_solution(15911203888531223163)
XLA Ops:
  0.6 58.9 %vcycle.1 = f32[2,3,8,4096]{3,2,1,0:T(8,128)} custom-call(f32[3,8,4096]{2,1,0:T(8,128)} %forcing_hbm.1, f32[8,4096]{1,0:T(8,128)} %viscosity_hbm.1, f32[1,24,384]{2,1,0:T(8,128)} %solver_hbm.1, s32[1,8]{1,0:T(1,128)} %bitcast.10, s32[1,32]{1,0:T(1,128)} %bitcast.11, s32[4,8]{1,0:T(4,128)} %bitcast.8, s32[2,8]{1,0:T(2,128)} %bitcast.9, s32[8,6]{1,0:T(8,128)} %hanging_hbm.1), custom_call_target="tpu_custom_call" | custom-call | tf_op jit(solution)/shard_map/vcycle/pallas_call | solution.py:810
  59.5 2.0 %slice_bitcast_fusion = (f32[3,8,4096]{2,1,0:T(8,128)}, f32[3,8,4096]{2,1,0:T(8,128)}) fusion(f32[2,3,8,4096]{3,2,1,0:T(8,128)} %vcycle.1), kind=kLoop, calls=%fused_computation | loop fusion | bytes 1572864 | tf_op jit(solution)/shard_map/squeeze | solution.py:887

commit v7 on v6

--- a/solution.py
+++ b/solution.py
@@ -376,7 +376,6 @@
 
     pl.semaphore_wait(barrier, n_mem - 1 + 2)
 
-    send(out_request, in_request, send_request, recv_request)
     for to in peers:
         pltpu.make_async_remote_copy(
             src_ref=out_face,
@@ -391,6 +390,7 @@
         out_plane[1, pl.ds(8 * v, 8), :] = effective[:, part(0, v)]
     for side in range(2):
         effective_plane(side).start()
+    send(out_request, in_request, send_request, recv_request)
     in_face[mem] = out_face[...]
     in_request[mem] = out_request[mem]
 

time: 61.9 us -> 62.2 us (level)
  no operation moved by 1% of the time
where the time goes in v7:
time: 62.2 us; the launch traced here: 61.9 us
  Pallas kernels  59.2 us (95%)
  local copies, waits for them, and re-layouts  2.04 us (3%)
  between operations  0.64 us (1%)
    pallas_call x1, Pallas kernels, local(): pl.pallas_call(functools.partial(kernel, n_grp, n_mem), out_shape=jax.Sha...  59.2 us
    squeeze x1, local copies, waits for them, and re-layouts, local(): return (both[0], both[1])  2.04 us

profile of v7, /device:TPU:0, one launch (start us, length us, event | category | flops | bytes accessed | tf_op | source)
XLA Modules:
  0.0 61.9 jit_solution(13465754397885449605)
XLA Ops:
  0.6 59.2 %vcycle.1 = f32[2,3,8,4096]{3,2,1,0:T(8,128)} custom-call(f32[3,8,4096]{2,1,0:T(8,128)} %forcing_hbm.1, f32[8,4096]{1,0:T(8,128)} %viscosity_hbm.1, f32[1,24,384]{2,1,0:T(8,128)} %solver_hbm.1, s32[1,8]{1,0:T(1,128)} %bitcast.10, s32[1,32]{1,0:T(1,128)} %bitcast.11, s32[4,8]{1,0:T(4,128)} %bitcast.8, s32[2,8]{1,0:T(2,128)} %bitcast.9, s32[8,6]{1,0:T(8,128)} %hanging_hbm.1), custom_call_target="tpu_custom_call" | custom-call | tf_op jit(solution)/shard_map/vcycle/pallas_call | solution.py:810
  59.8 2.0 %slice_bitcast_fusion = (f32[3,8,4096]{2,1,0:T(8,128)}, f32[3,8,4096]{2,1,0:T(8,128)}) fusion(f32[2,3,8,4096]{3,2,1,0:T(8,128)} %vcycle.1), kind=kLoop, calls=%fused_computation | loop fusion | bytes 1572864 | tf_op jit(solution)/shard_map/squeeze | solution.py:887
